TPU v7x, 32 devices: a whole 2x2x4 slice. The times are simulated.
32 devices in a mesh: dp: 8 (over z, y), row: 2 (over core), col: 2 (over x).
Axes of the slice: x: 2, y: 2, z: 4, core: 2. Of those that a mesh axis runs over, the one named last changes fastest.
Arguments:
- tokens_in: bfloat16 [2, 12608, 512], P(None, ('dp', 'col'), 'row'), may hold values from -6 to 6
- out_cotangent: bfloat16 [2, 12608, 512], P(None, ('dp', 'col'), 'row'), may hold values from -6 to 6
- expert_ids: int32 [2, 12608, 2], P(None, 'dp'), may hold values from 0 to 31, all different within a row; in each aligned block of 1576 rows (0 to 1575, 1576 to 3151, ..., all dimensions but the last counted through in order) at most 132 rows name the same one
- gate_values: float32 [2, 12608, 2], P(None, 'dp'), may hold values from 0.25 to 0.75
- first_gain: float32 [512], P('row'), may hold values from 0.5 to 1.5
- first_shift: float32 [512], P('row'), may hold values from -1.75 to 1.75
- second_gain: float32 [512], P('row'), may hold values from 0.5 to 1.5
- second_shift: float32 [512], P('row'), may hold values from -1.75 to 1.75
- qkv_weight: bfloat16 [512, 3, 512], P(('row', 'dp'), None, 'col'), may hold values from -0.25 to 0.25
- qkv_bias: float32 [2, 512], P(None, ('col', 'dp')), may hold values from -1.75 to 1.75
- proj_weight: bfloat16 [512, 512], P(('col', 'dp'), 'row'), may hold values from -0.5 to 0.5
- proj_bias: float32 [512], P(('row', 'dp')), may hold values from -1.75 to 1.75
- expand_weight: bfloat16 [32, 512, 2048], P('dp', 'row', 'col'), may hold values from -0.25 to 0.25
- expand_bias: float32 [32, 2048], P('row', ('col', 'dp')), may hold values from -1.75 to 1.75
- contract_weight: bfloat16 [32, 2048, 512], P('dp', 'col', 'row'), may hold values from -0.25 to 0.25
- contract_bias: float32 [32, 512], P(None, ('row', 'dp')), may hold values from -1.75 to 1.75
Outputs:
- layer_out: bfloat16 [2, 12608, 512], P(None, ('dp', 'col'), 'row')
- input_grad: float32 [2, 12608, 512], P(None, ('dp', 'col'), 'row')
- first_gain_grad: float32 [512], P('row')
- first_shift_grad: float32 [512], P('row')
- second_gain_grad: float32 [512], P('row')
- second_shift_grad: float32 [512], P('row')
- qkv_weight_grad: float32 [512, 3, 512], P(('row', 'dp'), None, 'col')
- qkv_bias_grad: float32 [2, 512], P(None, ('col', 'dp'))
- proj_weight_grad: float32 [512, 512], P(('col', 'dp'), 'row')
- proj_bias_grad: float32 [512], P(('row', 'dp'))
- expand_weight_grad: float32 [32, 512, 2048], P('dp', 'row', 'col')
- expand_bias_grad: float32 [32, 2048], P('row', ('col', 'dp'))
- contract_weight_grad: float32 [32, 2048, 512], P('dp', 'col', 'row')
- contract_bias_grad: float32 [32, 512], P(None, ('row', 'dp'))
Inputs may be any that keep to these rules, and one draw needn't show every extreme that they name: `expert_ids`: in each micro-batch, among the 1576 rows of one index of dp (aligned blocks of 1576 rows), no expert is named by more than 132 rows, a bound that some block reaches; a row names 2 different experts.
All inputs are finite; a program needn't handle non-finite values.
Results may differ from a plain program's by a relative error of at most 0.028.
Values may be sent and summed in bfloat16 or wider, within the bound.
No kernel may reach another device: no remote copies, remote signals or barrier semaphores. Data moves between devices by JAX's collectives and lax.ppermute only.
A program may use at most 320 MiB of HBM per device.

v0:
```python
import jax
import jax.numpy as jnp
from jax import lax
from jax.sharding import PartitionSpec as P

D = 512
HEADS = 8
EXPERTS = 32
TOP = 2
SEQ = 197


EPS = 1e-06
HIGH = lax.Precision.HIGHEST
ROOT_HALF = 0.7071067811865476
DENSITY = 0.3989422804014327


def fetch_blocks(
    qkv_weight,
    qkv_bias,
    proj_weight,
    proj_bias,
    expand_weight,
    expand_bias,
    contract_weight,
    contract_bias,
):
    return (
        lax.all_gather(qkv_weight, "dp", axis=0, tiled=True),
        lax.all_gather(qkv_bias.astype(jnp.bfloat16), "dp", axis=1, tiled=True).astype(
            qkv_bias.dtype
        ),
        lax.all_gather(proj_weight, "dp", axis=0, tiled=True),
        lax.all_gather(proj_bias.astype(jnp.bfloat16), "dp", axis=0, tiled=True).astype(
            proj_bias.dtype
        ),
        lax.all_gather(expand_weight, "dp", axis=0, tiled=True),
        lax.all_gather(expand_bias.astype(jnp.bfloat16), "dp", axis=1, tiled=True).astype(
            expand_bias.dtype
        ),
        lax.all_gather(contract_weight, "dp", axis=0, tiled=True),
        lax.all_gather(contract_bias.astype(jnp.bfloat16), "dp", axis=1, tiled=True).astype(
            contract_bias.dtype
        ),
    )


def feature_totals(first, second):
    return lax.psum((first, second), "row")


def token_rows(value):
    return lax.all_gather(value, "col", axis=0, tiled=True)


def hidden_sums(term, rows):
    return lax.psum_scatter(
        term(jnp.int32(0), rows * lax.axis_size("row")).astype(jnp.bfloat16),
        "row",
        scatter_dimension=0,
        tiled=True,
    ).astype(jnp.float32)


def hidden_rows(value):
    return lax.all_gather(value, "row", axis=0, tiled=True)


def token_sums(term, rows):
    return lax.psum_scatter(
        term(jnp.int32(0), rows * lax.axis_size("col")).astype(jnp.bfloat16),
        "col",
        scatter_dimension=0,
        tiled=True,
    ).astype(jnp.float32)


def grad_rows(value):
    return lax.all_gather(value, "col", axis=0, tiled=True)


def grad_hidden_sums(term, rows):
    return lax.psum_scatter(
        term(jnp.int32(0), rows * lax.axis_size("row")).astype(jnp.bfloat16),
        "row",
        scatter_dimension=0,
        tiled=True,
    ).astype(jnp.float32)


def grad_hidden_rows(value):
    return lax.all_gather(value, "row", axis=0, tiled=True)


def grad_token_sums(term, rows):
    return lax.psum_scatter(
        term(jnp.int32(0), rows * lax.axis_size("col")).astype(jnp.bfloat16),
        "col",
        scatter_dimension=0,
        tiled=True,
    ).astype(jnp.float32)


def part_of(array, start, count):
    return lax.dynamic_slice_in_dim(array, start, count, 0)


def norm_forward(value, gain, shift):
    first, second = feature_totals(
        jnp.sum(value, axis=-1, keepdims=True), jnp.sum(value * value, axis=-1, keepdims=True)
    )
    center = first / D
    spread = second / D - center * center
    factor = lax.rsqrt(spread + EPS)
    scaled = (value - center) * factor
    return (scaled * gain + shift, scaled, factor)


def norm_backward(grad, scaled, factor, gain):
    upper = grad * gain
    first, second = feature_totals(
        jnp.sum(upper, axis=-1, keepdims=True), jnp.sum(upper * scaled, axis=-1, keepdims=True)
    )
    return factor * (upper - first / D - scaled * second / D)


def destinations(routes, capacity):
    flat = routes.reshape(-1)
    labels = jnp.arange(EXPERTS, dtype=jnp.int32)
    onehot = (flat[:, None] == labels[None, :]).astype(jnp.int32)
    before = jnp.cumsum(onehot, axis=0) - onehot
    place = jnp.sum(before * onehot, axis=1)
    return (flat * capacity + place).reshape(routes.shape)


def expert_weights(routes, gates):
    labels = jnp.arange(EXPERTS, dtype=jnp.int32)
    return jnp.sum(gates[..., None] * (routes[..., None] == labels).astype(jnp.float32), axis=1)


def gelu_slope(value):
    return 0.5 * (1.0 + lax.erf(value * ROOT_HALF)) + value * DENSITY * jnp.exp(
        -0.5 * value * value
    )


def split_heads(triple_low):
    head_dim = D // HEADS
    images = triple_low.shape[0] // SEQ
    shaped = triple_low.reshape(images, SEQ, 3, triple_low.shape[2] // head_dim, head_dim)
    return (shaped[:, :, 0], shaped[:, :, 1], shaped[:, :, 2])


def attend(triple_low):
    scale = (D // HEADS) ** (-0.5)
    query, keys, values = split_heads(triple_low)
    scores = jnp.einsum("iqhd,ikhd->ihqk", query, keys, preferred_element_type=jnp.float32) * scale
    peak = jnp.max(scores, axis=-1, keepdims=True)
    expo = jnp.exp(scores - peak)
    total = jnp.sum(expo, axis=-1, keepdims=True)
    prob = (expo / total).astype(jnp.bfloat16)
    attended = jnp.einsum("ihqk,ikhd->iqhd", prob, values, preferred_element_type=jnp.float32)
    return (
        attended.reshape(triple_low.shape[0], triple_low.shape[2]).astype(jnp.bfloat16),
        peak + jnp.log(total),
    )


def attend_back(triple_low, logsum, attended_grad):
    scale = (D // HEADS) ** (-0.5)
    query, keys, values = split_heads(triple_low)
    scores = jnp.einsum("iqhd,ikhd->ihqk", query, keys, preferred_element_type=jnp.float32) * scale
    prob = jnp.exp(scores - logsum)
    upstream = attended_grad.reshape(values.shape)
    value_grad = jnp.einsum(
        "ihqk,iqhd->ikhd", prob.astype(jnp.bfloat16), upstream, preferred_element_type=jnp.float32
    )
    prob_grad = jnp.einsum("iqhd,ikhd->ihqk", upstream, values, preferred_element_type=jnp.float32)
    score_grad = (prob * (prob_grad - jnp.sum(prob * prob_grad, axis=-1, keepdims=True))).astype(
        jnp.bfloat16
    )
    query_grad = (
        jnp.einsum("ihqk,ikhd->iqhd", score_grad, keys, preferred_element_type=jnp.float32) * scale
    )
    key_grad = (
        jnp.einsum("ihqk,iqhd->ikhd", score_grad, query, preferred_element_type=jnp.float32) * scale
    )
    stacked = jnp.stack([query_grad, key_grad, value_grad], axis=2)
    return stacked.reshape(triple_low.shape)


def widened(array, axis_dim):
    shape = list(array.shape)
    shape[axis_dim] = shape[axis_dim] * lax.axis_size("dp")
    return jnp.zeros(tuple(shape), jnp.float32)


def on_device(
    tokens_in,
    out_cotangent,
    expert_ids,
    gate_values,
    first_gain,
    first_shift,
    second_gain,
    second_shift,
    qkv_weight,
    qkv_bias,
    proj_weight,
    proj_bias,
    expand_weight,
    expand_bias,
    contract_weight,
    contract_bias,
):
    micro = tokens_in.shape[0]
    local_rows = tokens_in.shape[1]
    group = expert_ids.shape[1]
    feature_ranks = lax.axis_size("row")
    hidden_tokens = group // feature_ranks
    experts_here = EXPERTS // feature_ranks
    capacity = (group * TOP * 4 + 3 * EXPERTS - 1) // (3 * EXPERTS)
    row_start = lax.axis_index("col") * local_rows
    sums = [
        widened(qkv_weight, 0),
        widened(qkv_bias, 1),
        widened(proj_weight, 0),
        widened(proj_bias, 0),
        widened(expand_weight, 0),
        widened(expand_bias, 1),
        widened(contract_weight, 0),
        widened(contract_bias, 1),
    ]
    norm_sums = [jnp.zeros(first_gain.shape, jnp.float32) for place in range(4)]
    held = None
    outputs = []
    in_grads = []
    for step in range(micro):
        held = fetch_blocks(
            qkv_weight,
            qkv_bias,
            proj_weight,
            proj_bias,
            expand_weight,
            expand_bias,
            contract_weight,
            contract_bias,
        )
        (
            qkv_full,
            qkv_shift,
            proj_full,
            proj_shift,
            expand_full,
            expand_shift,
            contract_full,
            contract_shift,
        ) = held
        routes = expert_ids[step]
        gates = gate_values[step]
        current = tokens_in[step].astype(jnp.float32)
        normed1, scaled1, factor1 = norm_forward(current, first_gain, first_shift)
        normed_rows = token_rows(normed1.astype(jnp.bfloat16))

        def qkv_term(start, count):
            return jnp.einsum(
                "td,dcf->tcf",
                part_of(normed_rows, start, count),
                qkv_full,
                preferred_element_type=jnp.float32,
            )

        triple = hidden_sums(qkv_term, hidden_tokens)
        offset = jnp.stack([qkv_shift[0], jnp.zeros_like(qkv_shift[0]), qkv_shift[1]])
        triple_low = (triple + offset[None]).astype(jnp.bfloat16)
        attended, logsum = attend(triple_low)
        attended_rows = hidden_rows(attended)

        def proj_term(start, count):
            return jnp.dot(
                part_of(attended_rows, start, count), proj_full, preferred_element_type=jnp.float32
            )

        middle = current + token_sums(proj_term, local_rows) + proj_shift
        normed2, scaled2, factor2 = norm_forward(middle, second_gain, second_shift)
        second_rows = token_rows(normed2.astype(jnp.bfloat16))
        target = destinations(routes, capacity)
        flat_target = target.reshape(-1)
        slots = jnp.zeros((EXPERTS * capacity, second_rows.shape[1]), jnp.bfloat16)
        slots = (
            slots.at[flat_target]
            .set(jnp.repeat(second_rows, TOP, axis=0))
            .reshape(EXPERTS, capacity, -1)
        )

        def expand_term(start, count):
            return jnp.einsum(
                "ecd,edh->ech",
                part_of(slots, start, count),
                part_of(expand_full, start, count),
                preferred_element_type=jnp.float32,
            )

        inner = hidden_sums(expand_term, experts_here) + expand_shift[:, None, :]
        active = jax.nn.gelu(inner, approximate=False).astype(jnp.bfloat16)
        active_rows = hidden_rows(active)
        outer = jnp.einsum(
            "ech,ehd->ecd", active_rows, contract_full, preferred_element_type=jnp.float32
        )
        outer = outer.reshape(EXPERTS * capacity, -1)

        def mix_term(start, count):
            picked = outer[part_of(target, start, count)]
            return jnp.sum(part_of(gates, start, count)[..., None] * picked, axis=1)

        mine = expert_weights(
            part_of(routes, row_start, local_rows), part_of(gates, row_start, local_rows)
        )
        bias_term = jnp.dot(mine, contract_shift, precision=HIGH)
        expert_out = token_sums(mix_term, local_rows) + bias_term
        outputs.append((middle + expert_out).astype(jnp.bfloat16))
        upstream = out_cotangent[step].astype(jnp.float32)
        upstream_rows = grad_rows(upstream.astype(jnp.bfloat16))
        upstream_wide = upstream_rows.astype(jnp.float32)
        sums[7] = sums[7] + jnp.dot(expert_weights(routes, gates).T, upstream_wide, precision=HIGH)
        placed = (gates[..., None] * upstream_wide[:, None, :]).reshape(-1, upstream_wide.shape[1])
        outer_grad = (
            jnp.zeros((EXPERTS * capacity, upstream_wide.shape[1]), jnp.float32)
            .at[flat_target]
            .set(placed)
        )
        outer_grad = outer_grad.astype(jnp.bfloat16).reshape(EXPERTS, capacity, -1)
        sums[6] = sums[6] + jnp.einsum(
            "ech,ecd->ehd", active_rows, outer_grad, preferred_element_type=jnp.float32
        )

        def active_term(start, count):
            return jnp.einsum(
                "ecd,ehd->ech",
                part_of(outer_grad, start, count),
                part_of(contract_full, start, count),
                preferred_element_type=jnp.float32,
            )

        active_grad = grad_hidden_sums(active_term, experts_here)
        inner_grad = (active_grad * gelu_slope(inner)).astype(jnp.bfloat16)
        sums[5] = sums[5] + jnp.sum(inner_grad.astype(jnp.float32), axis=1)
        inner_rows = grad_hidden_rows(inner_grad)
        sums[4] = sums[4] + jnp.einsum(
            "ecd,ech->edh", slots, inner_rows, preferred_element_type=jnp.float32
        )
        slot_grad = jnp.einsum(
            "ech,edh->ecd", inner_rows, expand_full, preferred_element_type=jnp.float32
        )
        slot_grad = slot_grad.reshape(EXPERTS * capacity, -1)

        def dispatch_term(start, count):
            return jnp.sum(slot_grad[part_of(target, start, count)], axis=1)

        normed2_grad = grad_token_sums(dispatch_term, local_rows)
        norm_sums[2] = norm_sums[2] + jnp.sum(normed2_grad * scaled2, axis=0)
        norm_sums[3] = norm_sums[3] + jnp.sum(normed2_grad, axis=0)
        middle_grad = upstream + norm_backward(normed2_grad, scaled2, factor2, second_gain)
        branch_rows = grad_rows(middle_grad.astype(jnp.bfloat16))
        sums[3] = sums[3] + jnp.sum(branch_rows.astype(jnp.float32), axis=0)
        sums[2] = sums[2] + jnp.einsum(
            "tf,td->fd", attended_rows, branch_rows, preferred_element_type=jnp.float32
        )

        def attended_term(start, count):
            return jnp.einsum(
                "td,fd->tf",
                part_of(branch_rows, start, count),
                proj_full,
                preferred_element_type=jnp.float32,
            )

        attended_grad = grad_hidden_sums(attended_term, hidden_tokens).astype(jnp.bfloat16)
        triple_grad = attend_back(triple_low, logsum, attended_grad).astype(jnp.bfloat16)
        triple_rows = grad_hidden_rows(triple_grad)
        column_sums = jnp.sum(triple_rows.astype(jnp.float32), axis=0)
        sums[1] = sums[1] + jnp.stack([column_sums[0], column_sums[2]])
        sums[0] = sums[0] + jnp.einsum(
            "td,tcf->dcf", normed_rows, triple_rows, preferred_element_type=jnp.float32
        )

        def normed_term(start, count):
            return jnp.einsum(
                "tcf,dcf->td",
                part_of(triple_rows, start, count),
                qkv_full,
                preferred_element_type=jnp.float32,
            )

        normed1_grad = grad_token_sums(normed_term, local_rows)
        norm_sums[0] = norm_sums[0] + jnp.sum(normed1_grad * scaled1, axis=0)
        norm_sums[1] = norm_sums[1] + jnp.sum(normed1_grad, axis=0)
        in_grads.append(middle_grad + norm_backward(normed1_grad, scaled1, factor1, first_gain))
    reduced = (
        lax.psum_scatter(
            sums[0].astype(jnp.bfloat16), "dp", scatter_dimension=0, tiled=True
        ).astype(jnp.float32),
        lax.psum_scatter(
            sums[1].astype(jnp.bfloat16), "dp", scatter_dimension=1, tiled=True
        ).astype(jnp.float32),
        lax.psum_scatter(
            sums[2].astype(jnp.bfloat16), "dp", scatter_dimension=0, tiled=True
        ).astype(jnp.float32),
        lax.psum_scatter(
            sums[3].astype(jnp.bfloat16), "dp", scatter_dimension=0, tiled=True
        ).astype(jnp.float32),
        lax.psum_scatter(
            sums[4].astype(jnp.bfloat16), "dp", scatter_dimension=0, tiled=True
        ).astype(jnp.float32),
        lax.psum_scatter(
            sums[5].astype(jnp.bfloat16), "dp", scatter_dimension=1, tiled=True
        ).astype(jnp.float32),
        lax.psum_scatter(
            sums[6].astype(jnp.bfloat16), "dp", scatter_dimension=0, tiled=True
        ).astype(jnp.float32),
        lax.psum_scatter(
            sums[7].astype(jnp.bfloat16), "dp", scatter_dimension=1, tiled=True
        ).astype(jnp.float32),
    )
    norm_total = lax.psum((norm_sums[0], norm_sums[1], norm_sums[2], norm_sums[3]), ("dp", "col"))
    return (
        jnp.stack(outputs),
        jnp.stack(in_grads),
        norm_total[0],
        norm_total[1],
        norm_total[2],
        norm_total[3],
        reduced[0],
        reduced[1],
        reduced[2],
        reduced[3],
        reduced[4],
        reduced[5],
        reduced[6],
        reduced[7],
    )


def solution(mesh):
    return jax.shard_map(
        on_device,
        mesh=mesh,
        in_specs=(
            P(None, ("dp", "col"), "row"),
            P(None, ("dp", "col"), "row"),
            P(None, "dp", None),
            P(None, "dp", None),
            P("row"),
            P("row"),
            P("row"),
            P("row"),
            P(("row", "dp"), None, "col"),
            P(None, ("col", "dp")),
            P(("col", "dp"), "row"),
            P(("row", "dp")),
            P("dp", "row", "col"),
            P("row", ("col", "dp")),
            P("dp", "col", "row"),
            P(None, ("row", "dp")),
        ),
        out_specs=(
            P(None, ("dp", "col"), "row"),
            P(None, ("dp", "col"), "row"),
            P("row"),
            P("row"),
            P("row"),
            P("row"),
            P(("row", "dp"), None, "col"),
            P(None, ("col", "dp")),
            P(("col", "dp"), "row"),
            P(("row", "dp")),
            P("dp", "row", "col"),
            P("row", ("col", "dp")),
            P("dp", "col", "row"),
            P(None, ("row", "dp")),
        ),
        check_vma=False,
    )
```

profile of v0, /device:TPU:0, one launch (start us, length us, event | category | flops | bytes accessed | tf_op | source)
XLA Modules:
  0.0 1945.9 jit_solution(3087480731314183705)
XLA Ops:
  15.9 13.2 all-gather.2
  30.2 31.8 %all_gather.81 = bf16[256,3,256]{2,0,1:T(8,128)(2,1)S(1)} all-gather(bf16[32,3,256]{2,0,1:T(8,128)(2,1)S(1)} %copy-done.101), channel_id=1, replica_groups=mesh['dp'=8,'row'=2,'col'=2] {'dp'}, dimensions={0}, use_global_device_ids=true | all-gather | bytes 442368 | tf_op jit(solution)/shard_map/all_gather | solution.py:30
  62.1 8.6 all-gather.6
  78.0 20.2 %all-gather.3 = bf16[8,32,2]{1,2,0:T(2,128)(2,1)S(1)} all-gather(bf16[1,32,2]{1,2,0:T(2,128)(2,1)S(1)} %convert_bitcast_fusion.4), channel_id=1, replica_groups=mesh['dp'=8,'row'=2,'col'=2] {'dp'}, dimensions={0}, use_global_device_ids=true | all-gather | bytes 1152 | tf_op jit(solution)/shard_map/all_gather | solution.py:31
  99.8 9.2 reduce-window.16
  111.8 32.1 %all_gather.84 = bf16[256,256]{1,0:T(8,128)(2,1)S(1)} all-gather(bf16[32,256]{1,0:T(8,128)(2,1)S(1)} %copy-done.107), channel_id=1, replica_groups=mesh['dp'=8,'row'=2,'col'=2] {'dp'}, dimensions={0}, use_global_device_ids=true | all-gather | bytes 147456 | tf_op jit(solution)/shard_map/all_gather | solution.py:34
  201.3 22.8 %fusion.224 = (bf16[792,256]{1,0:T(8,128)(2,1)S(1)}, bf16[792,256]{1,0:T(8,128)(2,1)S(1)}) fusion(bf16[1576,256]{1,0:T(8,128)(2,1)S(1)} %convolution_convert_fusion.9, bf16[1576,256]{1,0:T(8,128)(2,1)} %convolution_convert_fusion.8), kind=kCustom, calls=%all-reduce-scatter.12 | all-reduce-scatter fusion | flops 811009 | bytes 2425344
  230.0 17.8 all-reduce.2
  256.8 12.3 all-gather.8
  270.1 7.3 broadcast_in_dim.45
  282.1 19.6 %scatter_custom_fusion.1 = bf16[4224,256]{1,0:T(8,128)(2,1)} fusion(s32[3152]{0:T(1024)S(1)} %fusion.214, bf16[3152,256]{1,0:T(8,128)(2,1)} %reshape.369, bf16[]{:T(256)} %constant.49.clone.1), kind=kCustom, calls=%fused_computation.197 | custom fusion | bytes 2163200 | tf_op jit(solution)/shard_map/scatter | solution.py:293
  304.2 5.2 all-gather.20.cloned.1.call-done
  309.4 12.7 convolution_convert_fusion.2
  325.3 20.1 %all-gather.1 = bf16[1,1576,256]{2,0,1:T(2,128)(2,1)S(1)} all-gather(bf16[1,788,256]{2,0,1:T(2,128)(2,1)S(1)} %get-tuple-element.194), channel_id=3, replica_groups=mesh['dp'=8,'row'=2,'col'=2] {'col'}, dimensions={1}, use_global_device_ids=true | all-gather | bytes 1210368 | tf_op jit(solution)/shard_map/all_gather | solution.py:80
  346.6 5.5 mul.544
  352.1 5.4 mul.545
  358.8 28.7 %scatter_custom_fusion.3 = f32[4224,256]{1,0:T(8,128)} fusion(s32[3152]{0:T(1024)} %copy-done.109, f32[3152,256]{1,0:T(8,128)} %mul.545, f32[]{:T(128)} %constant.44.clone.1, f32[3152]{0:T(1024)S(1)} %mul.542), kind=kCustom, calls=%fused_computation.100 | custom fusion | flops 806912 | bytes 7566144 | tf_op jit(solution)/shard_map/scatter | solution.py:331
  393.9 143.3 %all-gather.24.cloned.1.call-done = bf16[32,1024,256]{2,1,0:T(8,128)(2,1)} async-done(((bf16[4,1024,256]{2,1,0:T(8,128)(2,1)}), bf16[32,1024,256]{2,1,0:T(8,128)(2,1)}) %all-gather.24.cloned.1.call-update) | async-done | bytes 16777232 | tf_op jit(solution)/shard_map/all_gather | solution.py:42
  537.2 11.2 convolution_convert_fusion
  550.3 9.2 reduce-window.14
  561.1 11.2 all-gather.5
  573.4 6.5 broadcast_in_dim.40
  581.5 19.6 %scatter_custom_fusion = bf16[4224,256]{1,0:T(8,128)(2,1)} fusion(s32[3152]{0:T(1024)S(1)} %fusion.213, bf16[3152,256]{1,0:T(8,128)(2,1)} %reshape.361, bf16[]{:T(256)} %constant.49.clone.1), kind=kCustom, calls=%fused_computation.199 | custom fusion | bytes 2163200 | tf_op jit(solution)/shard_map/scatter | solution.py:293
  603.6 12.6 convolution_convert_fusion.3
  617.3 19.1 all-gather
  637.7 5.4 mul.514
  643.1 5.4 mul.515
  649.2 28.7 %scatter_custom_fusion.2 = f32[4224,256]{1,0:T(8,128)} fusion(s32[3152]{0:T(1024)S(1)} %fusion.213, f32[3152,256]{1,0:T(8,128)} %mul.515, f32[]{:T(128)} %constant.44.clone.1, f32[3152]{0:T(1024)S(1)} %mul.512), kind=kCustom, calls=%fused_computation.102 | custom fusion | flops 806912 | bytes 7569412 | tf_op jit(solution)/shard_map/scatter | solution.py:331
  684.1 12.1 convolution_convert_fusion.1
  696.9 26.2 %all_gather.88 = bf16[16,1024]{1,0:T(8,128)(2,1)S(1)} all-gather(bf16[16,128]{1,0:T(8,128)(2,1)S(1)} %convert_element_type.334), channel_id=1, replica_groups=mesh['dp'=8,'row'=2,'col'=2] {'dp'}, dimensions={1}, use_global_device_ids=true | all-gather | bytes 36864 | tf_op jit(solution)/shard_map/all_gather | solution.py:39
  723.2 52.4 %convert_reduce_fusion = (f32[16,1024]{1,0:T(8,128)S(1)}, bf16[16,132,1024]{2,1,0:T(8,128)(2,1)}, bf16[16,132,1024]{2,1,0:T(8,128)(2,1)}, bf16[16,132,1024]{2,1,...) fusion(f32[16,1024]{1,0:T(8,128)S(1)} %convert_element_type.335, ...), kind=kLoop, calls=%fused_computation.30 | loop fusion | flops 345997312 | bytes 34799616 | tf_op jit(solution)/shard_map/reduce_sum | solution.py:348
  780.0 6.9 copy.384
  799.2 13.7 fusion.51
  813.0 5.3 reshape.314
  818.2 9.7 gather_fusion.2
  831.1 10.6 reduce_sum.424
  841.6 13.9 fusion.47
  855.5 4.9 reshape.317
  860.5 9.7 gather_fusion.3
  873.4 10.7 reduce_sum.430
  884.1 23.9 %fusion.223 = (bf16[792,256]{1,0:T(8,128)(2,1)}, bf16[792,256]{1,0:T(8,128)(2,1)}) fusion(bf16[1576,256]{1,0:T(8,128)(2,1)} %reduce_sum.424, bf16[1576,256]{1,0:T(8,128)(2,1)} %reduce_sum.430), kind=kCustom, calls=%all-reduce-scatter.11 | all-reduce-scatter fusion | flops 811009 | bytes 2425344
  933.4 12.4 all-gather.10
  947.3 11.7 all-gather.9
  962.7 5.9 fusion.225
  1025.7 6.7 copy.348
  1032.5 7.2 copy.362
  1048.4 34.9 %fusion.49 = f32[32,256,1024]{2,1,0:T(8,128)} fusion(bf16[32,132,256]{2,1,0:T(8,128)(2,1)S(1)} %copy-done.11, bf16[32,132,1024]{2,0,1:T(8,128)(2,1)} %all-gather.28.cloned.1.call-done), kind=kOutput, calls=%fused_computation.71 | convolution fusion | flops 2214592512 | bytes 44367872 | tf_op jit(solution)/shard_map/ecd,ech->edh/dot_general | solution.py:350
  1103.2 35.4 %add_convert_fusion.1 = bf16[32,256,1024]{2,1,0:T(8,128)(2,1)} fusion(f32[32,256,1024]{2,1,0:T(8,128)} %fusion.49, bf16[32,132,256]{2,1,0:T(8,128)(2,1)S(1)} %copy-done.13, bf16[32,132,1024]{2,0,1:T(8,128)(2,1)} %all-gather.32.cloned.1.call-done), kind=kOutput, calls=%fused_computation.9 | convolution fusion | flops 2231369728 | bytes 61145088 | tf_op jit(solution)/shard_map/ecd,ech->edh/dot_general | solution.py:350
  1140.2 21.7 %fusion.56 = f32[32,1024,256]{2,1,0:T(8,128)} fusion(bf16[32,132,256]{2,1,0:T(8,128)(2,1)S(1)} %copy-done.9, bf16[32,132,1024]{2,0,1:T(8,128)(2,1)} %all-gather.22.cloned.1.call-done), kind=kOutput, calls=%fused_computation.78 | convolution fusion | flops 2214592512 | bytes 44367872 | tf_op jit(solution)/shard_map/ech,ecd->ehd/dot_general | solution.py:334
  1161.9 23.8 %add_convert_fusion = bf16[32,1024,256]{2,1,0:T(8,128)(2,1)} fusion(f32[32,1024,256]{2,1,0:T(8,128)} %fusion.56, bf16[32,132,256]{2,1,0:T(8,128)(2,1)} %copy-done.14, bf16[32,132,1024]{2,0,1:T(8,128)(2,1)} %all-gather.26.cloned.1.call-done), kind=kOutput, calls=%fused_computation.8 | convolution fusion | flops 2231369728 | bytes 61145088 | tf_op jit(solution)/shard_map/ech,ecd->ehd/dot_general | solution.py:334
  1189.4 31.0 %all_gather.91 = bf16[32,256]{0,1:T(8,128)(2,1)S(1)} all-gather(bf16[32,32]{0,1:T(8,128)(2,1)S(1)} %copy.351), channel_id=1, replica_groups=mesh['dp'=8,'row'=2,'col'=2] {'dp'}, dimensions={1}, use_global_device_ids=true | all-gather | bytes 18432 | tf_op jit(solution)/shard_map/all_gather | solution.py:43
  1226.3 16.3 fusion.54
  1242.6 5.1 reshape.312
  1247.6 9.7 gather_fusion.1
  1260.4 16.3 fusion.58
  1276.8 4.9 reshape.306
  1281.7 9.7 gather_fusion
  1294.5 11.4 multiply_reduce_fusion.2
  1305.9 10.7 multiply_reduce_fusion.3
  1317.1 21.3 %all-reduce.15 = bf16[256]{0:T(256)(128)(2,1)S(1)} all-reduce(bf16[256]{0:T(256)(128)(2,1)S(1)} %add_convert_fusion.9), channel_id=23, replica_groups=mesh['dp'=8,'row'=2,'col'=2] {'dp'}, use_global_device_ids=true, to_apply=%region_89.90.clone | all-reduce | flops 256 | bytes 1024
  1343.2 31.7 %fusion.222 = (bf16[792,256]{1,0:T(8,128)(2,1)}, bf16[792,256]{1,0:T(8,128)(2,1)S(1)}, bf16[792,256]{1,0:T(8,128)(2,1)}, bf16[792,256]{1,0:T(8,128)(2,1)}) fusion(bf16[1576,256]{1,0:T(8,128)(2,1)S(1)} %copy-done.61, bf16[1576,256]{1,0:T(8,128)(2,1)S(1)} %copy-done.62, bf16[1576,256]{1,0:T(8,128)(2,1)} %fusion.67, bf16[1576,256]{1,0:T(8,128)(2,1)} %fusion.66), kind=kCustom, calls=%all-reduce-scatter.10 | all-reduce-scatter fusion | flops 1622017 | bytes 4850176
  1411.2 39.3 %all-reduce.26 = (f32[256]{0:T(256)}, f32[256]{0:T(256)}, f32[256]{0:T(256)}, f32[256]{0:T(256)}) all-reduce(f32[256]{0:T(256)S(1)} %add.398, f32[256]{0:T(256)S(1)} %add.399, f32[256]{0:T(256)S(1)} %add.400, f32[256]{0:T(256)S(1)} %add.401), channel_id=1, replica_groups=mesh['dp'=8,'row'=2,'col'=2] {'dp','col'}, use_global_device_ids=true, to_apply=%region_72.73 | all-reduce | flops 1024 | bytes 8192 | tf_op jit(solution)/shard_map/psum | solution.py:426
  1452.0 199.5 %reduce-scatter.52.cloned.1.call-done = bf16[4,256,1024]{2,1,0:T(8,128)(2,1)} async-done(((bf16[32,256,1024]{2,1,0:T(8,128)(2,1)}), bf16[4,256,1024]{2,1,0:T(8,128)(2,1)}) %reduce-scatter.52.cloned.1.call-update) | async-done | bytes 2097168 | tf_op jit(solution)/shard_map/reduce_scatter | solution.py:413
  1655.5 278.5 %reduce-scatter.54.cloned.1.call-done = bf16[4,1024,256]{2,1,0:T(8,128)(2,1)} async-done(((bf16[32,1024,256]{2,1,0:T(8,128)(2,1)}), bf16[4,1024,256]{2,1,0:T(8,128)(2,1)}) %reduce-scatter.54.cloned.1.call-update) | async-done | bytes 2097168 | tf_op jit(solution)/shard_map/reduce_scatter | solution.py:419
  (578 shorter events, 334.4 us)
Async XLA Ops:
  8.0 136.0 %all-reduce.38.cloned.1.call-start = ((), (), s32[]{:S(2)}) async-start(), calls=%async_computation.30 | async-start | bytes 9682944
  11.2 244.9 %copy-start.15 = (bf16[1,788,256]{2,1,0:T(8,128)(2,1)}, bf16[1,788,256]{2,1,0:T(8,128)(2,1)S(1)}, u32[]{:S(2)}) copy-start(bf16[1,788,256]{2,1,0:T(8,128)(2,1)S(1)} %get-tuple-element.185) | copy-start | bytes 1210372
  11.3 244.9 %copy-start.18 = (bf16[1,788,256]{2,1,0:T(8,128)(2,1)}, bf16[1,788,256]{2,1,0:T(8,128)(2,1)S(1)}, u32[]{:S(2)}) copy-start(bf16[1,788,256]{2,1,0:T(8,128)(2,1)S(1)} %get-tuple-element.244) | copy-start | bytes 1210372
  15.3 46.7 %copy-start.89 = (f32[788]{0:T(1024)}, f32[788]{0:T(1024)S(1)}, u32[]{:S(2)}) copy-start(f32[788]{0:T(1024)S(1)} %get-tuple-element.124) | copy-start | bytes 9460
  15.3 46.7 %copy-start.91 = (f32[788]{0:T(1024)}, f32[788]{0:T(1024)S(1)}, u32[]{:S(2)}) copy-start(f32[788]{0:T(1024)S(1)} %get-tuple-element.125) | copy-start | bytes 9460
  15.4 46.7 %copy-start.85 = (f32[788]{0:T(1024)}, f32[788]{0:T(1024)S(1)}, u32[]{:S(2)}) copy-start(f32[788]{0:T(1024)S(1)} %get-tuple-element.120) | copy-start | bytes 9460
  15.4 46.7 %copy-start.87 = (f32[788]{0:T(1024)}, f32[788]{0:T(1024)S(1)}, u32[]{:S(2)}) copy-start(f32[788]{0:T(1024)S(1)} %get-tuple-element.121) | copy-start | bytes 9460
  76.8 232.7 %all-gather.20.cloned.1.call-start = ((), (), s32[]{:S(2)}) async-start(), calls=%async_computation.11 | async-start | bytes 18874368 | tf_op jit(solution)/shard_map/all_gather | solution.py:38
  77.3 459.8 %all-gather.24.cloned.1.call-start = ((), (), s32[]{:S(2)}) async-start(), calls=%async_computation.14 | async-start | bytes 18874368 | tf_op jit(solution)/shard_map/all_gather | solution.py:42
  77.9 645.2 %reduce-scatter.42.cloned.1.call-start = ((), (), s32[]{:S(2)}) async-start(), calls=%async_computation.15 | async-start | bytes 13369344 | tf_op jit(solution)/shard_map/reduce_scatter | solution.py:58
  98.6 695.5 %copy-start.21 = (s32[1,1576,2]{2,1,0:T(8,128)}, s32[1,1576,2]{2,1,0:T(8,128)S(1)}, u32[]{:S(2)}) copy-start(s32[1,1576,2]{2,1,0:T(8,128)S(1)} %copy.450) | copy-start | bytes 37828
  143.9 55.0 %copy-start.55 = (bf16[256,256]{1,0:T(8,128)(2,1)}, bf16[256,256]{1,0:T(8,128)(2,1)S(1)}, u32[]{:S(2)}) copy-start(bf16[256,256]{1,0:T(8,128)(2,1)S(1)} %all_gather.84) | copy-start | bytes 393220
  193.9 53.9 %copy-start.123 = (u32[32]{0:T(128)S(1)}, u32[32]{0:T(128)}, u32[]{:S(2)}) copy-start(u32[32]{0:T(128)} %constant.148) | copy-start | bytes 388
  197.3 58.8 %copy-start.112 = (f32[256]{0:T(256)S(1)}, f32[256]{0:T(256)}, u32[]{:S(2)}) copy-start(f32[256]{0:T(256)} %param.22) | copy-start | bytes 3076
  197.3 58.8 %copy-start.121 = (f32[256]{0:T(256)S(1)}, f32[256]{0:T(256)}, u32[]{:S(2)}) copy-start(f32[256]{0:T(256)} %param.23) | copy-start | bytes 3076
  224.1 24.9 %collective-permute-start = (bf16[4,256]{1,0:T(4,128)(2,1)S(1)}, bf16[4,256]{1,0:T(4,128)(2,1)S(1)}, u32[]{:S(2)}, u32[]{:S(2)}) collective-permute-start(bf16[4,256]{1,0:T(4,128)(2,1)S(1)} %slice.138), channel_id=1, source_target_pairs={{0,1},{2,3},{4,5},{6,7},{8,9},{10,11},{12,13},{14,15},{16,17},{18,... | collective-permute-start | bytes 6152
  227.5 23.0 %collective-permute-start.2 = (bf16[4,256]{1,0:T(4,128)(2,1)S(1)}, bf16[4,256]{1,0:T(4,128)(2,1)S(1)}, u32[]{:S(2)}, u32[]{:S(2)}) collective-permute-start(bf16[4,256]{1,0:T(4,128)(2,1)S(1)} %slice.140), channel_id=1, source_target_pairs={{0,1},{2,3},{4,5},{6,7},{8,9},{10,11},{12,13},{14,15},{16,17},{18,... | collective-permute-start | bytes 6152
  229.0 53.0 %copy-start.109 = (s32[3152]{0:T(1024)}, s32[3152]{0:T(1024)S(1)}, u32[]{:S(2)}) copy-start(s32[3152]{0:T(1024)S(1)} %fusion.214) | copy-start | bytes 37828
  322.1 401.0 %reduce-scatter.46.cloned.1.call-start = ((), (), s32[]{:S(2)}) async-start(), calls=%async_computation.20 | async-start | bytes 13369344 | tf_op jit(solution)/shard_map/reduce_scatter | solution.py:84
  358.1 290.3 %copy-start.78 = (f32[1,1576,2]{1,2,0:T(2,128)}, f32[1,1576,2]{1,2,0:T(2,128)S(1)}, u32[]{:S(2)}) copy-start(f32[1,1576,2]{1,2,0:T(2,128)S(1)} %get-tuple-element.205) | copy-start | bytes 37828
  393.9 154.5 %copy-start.14 = (bf16[32,132,256]{2,1,0:T(8,128)(2,1)}, bf16[32,132,256]{2,1,0:T(8,128)(2,1)S(1)}, u32[]{:S(2)}) copy-start(bf16[32,132,256]{2,1,0:T(8,128)(2,1)S(1)} %reshape.316) | copy-start | bytes 6488068
  548.4 174.7 %reduce-scatter.40.cloned.1.call-start = ((), (), s32[]{:S(2)}) async-start(), calls=%async_computation.12 | async-start | bytes 13369344 | tf_op jit(solution)/shard_map/reduce_scatter | solution.py:58
  616.2 107.0 %reduce-scatter.44.cloned.1.call-start = ((), (), s32[]{:S(2)}) async-start(), calls=%async_computation.17 | async-start | bytes 13369344 | tf_op jit(solution)/shard_map/reduce_scatter | solution.py:84
  696.2 103.0 %all-gather.28.cloned.1.call-start = ((), (), s32[]{:S(2)}) async-start(), calls=%async_computation.18 | async-start | bytes 12976128 | tf_op jit(solution)/shard_map/all_gather | solution.py:93
  780.0 61.6 %all-gather.32.cloned.1.call-start = ((), (), s32[]{:S(2)}) async-start(), calls=%async_computation.21 | async-start | bytes 12976128 | tf_op jit(solution)/shard_map/all_gather | solution.py:93
  787.0 301.0 %all-gather.30.cloned.1.call-start = ((), (), s32[]{:S(2)}) async-start(), calls=%async_computation.19 | async-start | bytes 4841472 | tf_op jit(solution)/shard_map/all_gather | solution.py:93
  794.7 65.8 %copy-start.2 = (s32[4096]{0:T(1024)}, s32[4096]{0:T(1024)S(1)}, u32[]{:S(2)}) copy-start(s32[4096]{0:T(1024)S(1)} %pad_clamp_fusion) | copy-start | bytes 49156
  873.4 49.3 %copy-start.16 = (bf16[1,788,256]{2,1,0:T(8,128)(2,1)S(1)}, bf16[1,788,256]{2,1,0:T(8,128)(2,1)}, u32[]{:S(2)}) copy-start(bf16[1,788,256]{2,1,0:T(8,128)(2,1)} %copy-done.15) | copy-start | bytes 1210372
  873.4 49.3 %copy-start.19 = (bf16[1,788,256]{2,1,0:T(8,128)(2,1)S(1)}, bf16[1,788,256]{2,1,0:T(8,128)(2,1)}, u32[]{:S(2)}) copy-start(bf16[1,788,256]{2,1,0:T(8,128)(2,1)} %copy-done.18) | copy-start | bytes 1210372
  873.4 49.3 %copy-start.28 = (bf16[796,256]{1,0:T(8,128)(2,1)S(1)}, bf16[796,256]{1,0:T(8,128)(2,1)}, u32[]{:S(2)}) copy-start(bf16[796,256]{1,0:T(8,128)(2,1)} %copy-done.27) | copy-start | bytes 1222660
  873.4 49.3 %copy-start.31 = (bf16[796,256]{1,0:T(8,128)(2,1)S(1)}, bf16[796,256]{1,0:T(8,128)(2,1)}, u32[]{:S(2)}) copy-start(bf16[796,256]{1,0:T(8,128)(2,1)} %copy-done.30) | copy-start | bytes 1222660
  873.4 49.3 %copy-start.94 = (f32[788]{0:T(1024)S(1)}, f32[788]{0:T(1024)}, u32[]{:S(2)}) copy-start(f32[788]{0:T(1024)} %copy-done.93) | copy-start | bytes 9460
  873.4 49.3 %copy-start.96 = (f32[788]{0:T(1024)S(1)}, f32[788]{0:T(1024)}, u32[]{:S(2)}) copy-start(f32[788]{0:T(1024)} %copy-done.95) | copy-start | bytes 9460
  873.4 49.3 %copy-start.98 = (f32[788]{0:T(1024)S(1)}, f32[788]{0:T(1024)}, u32[]{:S(2)}) copy-start(f32[788]{0:T(1024)} %copy-done.97) | copy-start | bytes 9460
  873.4 49.3 %copy-start.100 = (f32[788]{0:T(1024)S(1)}, f32[788]{0:T(1024)}, u32[]{:S(2)}) copy-start(f32[788]{0:T(1024)} %copy-done.99) | copy-start | bytes 9460
  873.4 49.3 %copy-start.103 = (f32[256]{0:T(256)S(1)}, f32[256]{0:T(256)}, u32[]{:S(2)}) copy-start(f32[256]{0:T(256)} %copy-done.102) | copy-start | bytes 3076
  873.4 49.3 %copy-start.113 = (f32[256]{0:T(256)S(1)}, f32[256]{0:T(256)}, u32[]{:S(2)}) copy-start(f32[256]{0:T(256)} %param.22) | copy-start | bytes 3076
  908.8 6.3 collective-permute-start.4
  913.1 5.8 collective-permute-start.7
  969.3 2.8 collective-permute-start.5
  995.2 96.5 %all-gather.34.cloned.1.call-start = ((), (), s32[]{:S(2)}) async-start(), calls=%async_computation.22 | async-start | bytes 4841472 | tf_op jit(solution)/shard_map/all_gather | solution.py:93
  996.0 3.0 collective-permute-start.8
  1025.6 113.5 %all-gather.22.cloned.1.call-start = ((), (), s32[]{:S(2)}) async-start(), calls=%async_computation.13 | async-start | bytes 12976128 | tf_op jit(solution)/shard_map/all_gather | solution.py:67
  1032.4 129.5 %all-gather.26.cloned.1.call-start = ((), (), s32[]{:S(2)}) async-start(), calls=%async_computation.16 | async-start | bytes 12976128 | tf_op jit(solution)/shard_map/all_gather | solution.py:67
  1039.7 183.7 %reduce-scatter.60.cloned.1.call-start = ((), (), s32[]{:S(2)}) async-start(), calls=%async_computation.29 | async-start | bytes 73728
  1047.3 177.6 %reduce-scatter.58.cloned.1.call-start = ((), (), s32[]{:S(2)}) async-start(), calls=%async_computation.28 | async-start | bytes 294912
  1048.2 333.3 %reduce-scatter.50.cloned.1.call-start = ((), (), s32[]{:S(2)}) async-start(), calls=%async_computation.24 | async-start | bytes 147456 | tf_op jit(solution)/shard_map/reduce_scatter | solution.py:407
  1087.8 322.1 %reduce-scatter.56.cloned.1.call-start = ((), (), s32[]{:S(2)}) async-start(), calls=%async_computation.27 | async-start | bytes 73728
  1096.2 354.4 %reduce-scatter.48.cloned.1.call-start = ((), (), s32[]{:S(2)}) async-start(), calls=%async_computation.23 | async-start | bytes 442368 | tf_op jit(solution)/shard_map/reduce_scatter | solution.py:401
  1103.1 548.3 %reduce-scatter.52.cloned.1.call-start = ((), (), s32[]{:S(2)}) async-start(), calls=%async_computation.25 | async-start | bytes 18874368 | tf_op jit(solution)/shard_map/reduce_scatter | solution.py:413
  1138.6 795.4 %reduce-scatter.54.cloned.1.call-start = ((), (), s32[]{:S(2)}) async-start(), calls=%async_computation.26 | async-start | bytes 18874368 | tf_op jit(solution)/shard_map/reduce_scatter | solution.py:419
  1343.1 47.3 %copy-start.17 = (bf16[1,788,256]{2,1,0:T(8,128)(2,1)S(1)}, bf16[1,788,256]{2,1,0:T(8,128)(2,1)}, u32[]{:S(2)}) copy-start(bf16[1,788,256]{2,1,0:T(8,128)(2,1)} %copy-done.15) | copy-start | bytes 1210372
  1343.1 47.3 %copy-start.20 = (bf16[1,788,256]{2,1,0:T(8,128)(2,1)S(1)}, bf16[1,788,256]{2,1,0:T(8,128)(2,1)}, u32[]{:S(2)}) copy-start(bf16[1,788,256]{2,1,0:T(8,128)(2,1)} %copy-done.18) | copy-start | bytes 1210372
  1343.1 47.3 %copy-start.86 = (f32[788]{0:T(1024)S(1)}, f32[788]{0:T(1024)}, u32[]{:S(2)}) copy-start(f32[788]{0:T(1024)} %copy-done.85) | copy-start | bytes 9460
  1343.1 47.3 %copy-start.88 = (f32[788]{0:T(1024)S(1)}, f32[788]{0:T(1024)}, u32[]{:S(2)}) copy-start(f32[788]{0:T(1024)} %copy-done.87) | copy-start | bytes 9460
  1343.2 47.3 %copy-start.90 = (f32[788]{0:T(1024)S(1)}, f32[788]{0:T(1024)}, u32[]{:S(2)}) copy-start(f32[788]{0:T(1024)} %copy-done.89) | copy-start | bytes 9460
  1343.2 47.3 %copy-start.92 = (f32[788]{0:T(1024)S(1)}, f32[788]{0:T(1024)}, u32[]{:S(2)}) copy-start(f32[788]{0:T(1024)} %copy-done.91) | copy-start | bytes 9460
  1343.2 47.3 %copy-start.111 = (f32[256]{0:T(256)S(1)}, f32[256]{0:T(256)}, u32[]{:S(2)}) copy-start(f32[256]{0:T(256)} %param.20) | copy-start | bytes 3076
  1343.2 59.8 %copy-start.32 = (bf16[796,256]{1,0:T(8,128)(2,1)S(1)}, bf16[796,256]{1,0:T(8,128)(2,1)}, u32[]{:S(2)}) copy-start(bf16[796,256]{1,0:T(8,128)(2,1)} %copy-done.30) | copy-start | bytes 1222660
  1343.2 59.8 %copy-start.104 = (f32[256]{0:T(256)S(1)}, f32[256]{0:T(256)}, u32[]{:S(2)}) copy-start(f32[256]{0:T(256)} %copy-done.102) | copy-start | bytes 3076
  1375.6 10.6 collective-permute-start.6
  1379.6 8.7 collective-permute-start.9
  1383.5 8.2 collective-permute-start.3
  1384.8 10.7 collective-permute-start.1
  (92 other events, 1192.0 us)
Sparse Core Ops, SparseCore 0:
  76.9 30.0 all-reduce.37
  322.2 15.4 reduce-scatter.41
  548.5 15.4 reduce-scatter.45
  616.3 16.0 reduce-scatter.39
  696.3 16.9 reduce-scatter.43
  780.1 19.0 all-gather.27
  800.9 22.0 all-gather.31
  995.4 12.6 all-gather.29
  1025.7 12.6 all-gather.33
  1039.9 22.0 all-gather.21
  1063.6 22.0 all-gather.25
Sparse Core Ops, SparseCore 1:
  79.6 229.8 all-gather.19
  311.6 225.5 all-gather.23
  1047.3 61.6 reduce-scatter.59
  1113.3 60.4 reduce-scatter.57
  1177.5 59.9 reduce-scatter.49
  1241.8 60.4 reduce-scatter.55
  1305.8 61.2 reduce-scatter.47
  1371.2 280.2 reduce-scatter.51
  1655.1 278.9 reduce-scatter.53
where the time goes:
time: 1960 us; the launch traced here: 1950 us
  waiting for transfers between devices  633 us (32%)
  blocking collectives  431 us (22%)
  local copies, waits for them, and re-layouts  331 us (17%)
  matrix products  277 us (14%)
  other arithmetic  227 us (12%)
  starting transfers between devices  24.3 us (1%)
  between operations  21.7 us (1%)
    reduce_scatter x1, waiting for transfers between devices, on_device(): lax.psum_scatter(sums[6].astype(jnp.bfloat16), 'dp', scatter_dimension=0,...  279 us
    reduce_scatter x1, waiting for transfers between devices, on_device(): lax.psum_scatter(sums[4].astype(jnp.bfloat16), 'dp', scatter_dimension=0,...  199 us
    all_gather x1, waiting for transfers between devices, fetch_blocks(): lax.all_gather(contract_weight, 'dp', axis=0, tiled=True)  143 us
    unnamed x6, blocking collectives  123 us
    unnamed x309, local copies, waits for them, and re-layouts  86.8 us
    dot_general x2, matrix products, on_device(): jnp.einsum('ecd,ech->edh', slots, inner_rows, preferred_element_type=jnp....  70.2 us
    all_gather x4, blocking collectives, grad_rows(): return lax.all_gather(value, 'col', axis=0, tiled=True)  63.3 us
    scatter x2, other arithmetic, on_device(): outer_grad = jnp.zeros((EXPERTS * capacity, upstream_wide.shape[1]), jnp....  57.4 us
  transfers between devices with their start and end apart: 30, of which 7 were waited for; matrix products, arithmetic and copies ran while one was open for 37% of the time, Pallas kernels for 0%

commit v1 on v0

v1 whole, which is shorter than its diff:
```python
import functools

import jax
import jax.numpy as jnp
from jax import lax
from jax.experimental import pallas as pl
from jax.experimental.pallas import tpu as pltpu
from jax.sharding import PartitionSpec as P

D = 512
HEADS = 8
EXPERTS = 32
TOP = 2
SEQ = 197
HEAD_DIM = D // HEADS
PAIR = 2 * HEAD_DIM
PAD = 208

EPS = 1e-06
HIGH = lax.Precision.HIGHEST
ROOT_HALF = 0.7071067811865476
DENSITY = 0.3989422804014327
SCALE = HEAD_DIM ** (-0.5)
FAR = -1e30
MIB = 1 << 20

BF16 = jnp.bfloat16
F32 = jnp.float32


def round_up(value, unit):
    return (value + unit - 1) // unit * unit


def swap(value, axis, bit=1):
    size = lax.axis_size(axis)
    return lax.ppermute(value, axis, [(place, place ^ bit) for place in range(size)])


def either(first, when_true, when_false):
    return jnp.where(first, when_true, when_false)


def in_order(index, own, other, axis):
    return jnp.where(
        index == 0,
        jnp.concatenate([own, other], axis),
        jnp.concatenate([other, own], axis),
    )


def chosen(array, index, axis=0):
    return lax.dynamic_index_in_dim(array, index, axis, keepdims=False)


def contract(left, right, left_dim, right_dim):
    return lax.dot_general(
        left, right, (((left_dim,), (right_dim,)), ((), ())), preferred_element_type=F32
    )


def call(kernel, grid, in_specs, out_specs, out_shape, scratch=(), limit=48):
    return pl.pallas_call(
        kernel,
        grid=grid,
        in_specs=in_specs,
        out_specs=out_specs,
        out_shape=out_shape,
        scratch_shapes=list(scratch),
        compiler_params=pltpu.CompilerParams(
            dimension_semantics=("arbitrary",) * len(grid), vmem_limit_bytes=limit * MIB
        ),
    )


def whole(shape):
    return pl.BlockSpec(shape, lambda *_: (0,) * len(shape))


def stepped(shape, axis=0):
    return pl.BlockSpec(
        shape, lambda g: tuple(g if place == axis else 0 for place in range(len(shape)))
    )


def destinations(routes, capacity):
    labels = jnp.arange(EXPERTS, dtype=jnp.int32)
    named = (routes[:, :, None] == labels).astype(F32)
    count = routes.shape[0]
    place = jnp.arange(count, dtype=jnp.int32)
    earlier = (place[None, :] < place[:, None]).astype(BF16)
    before = jnp.dot(earlier, named.sum(axis=1).astype(BF16), preferred_element_type=F32)
    return jnp.sum(before[:, None, :] * named, axis=2).astype(jnp.int32)


def dispatch_kernel(gated, target_ref, gate_ref, own_ref, other_ref, out_ref):
    rows = out_ref.shape[0]
    count = own_ref.shape[0]
    place = lax.broadcasted_iota(jnp.int32, (rows, count), 0) + pl.program_id(0) * rows
    total = None
    for half, tokens in ((0, own_ref), (1, other_ref)):
        first = place == target_ref[2 * half : 2 * half + 1, :]
        second = place == target_ref[2 * half + 1 : 2 * half + 2, :]
        if gated:
            weight = jnp.where(
                first,
                gate_ref[2 * half : 2 * half + 1, :],
                jnp.where(second, gate_ref[2 * half + 1 : 2 * half + 2, :], 0.0),
            )
        else:
            weight = jnp.where(first | second, 1.0, 0.0)
        term = jnp.dot(weight.astype(BF16), tokens[...], preferred_element_type=F32)
        total = term if total is None else total + term
    out_ref[...] = total.astype(BF16)


def dispatch(target_rows, gate_rows, own, other, rows, gated):
    steps = 4
    return call(
        functools.partial(dispatch_kernel, gated),
        (steps,),
        [whole(target_rows.shape), whole(gate_rows.shape), whole(own.shape), whole(other.shape)],
        stepped((rows // steps, D)),
        jax.ShapeDtypeStruct((rows, D), BF16),
    )(target_rows, gate_rows, own, other)


def combine_kernel(gated, target_ref, gate_ref, slots_ref, out_ref):
    count, rows = out_ref.shape[0], slots_ref.shape[0]
    place = lax.broadcasted_iota(jnp.int32, (count, rows), 1)
    first = place == target_ref[:, 0:1]
    second = place == target_ref[:, 1:2]
    if gated:
        weight = jnp.where(first, gate_ref[:, 0:1], jnp.where(second, gate_ref[:, 1:2], 0.0))
    else:
        weight = jnp.where(first | second, 1.0, 0.0)
    out = jnp.dot(weight.astype(BF16), slots_ref[...], preferred_element_type=F32)
    out_ref[...] = out.astype(out_ref.dtype)


def combine(target_columns, gate_columns, slots, gated, dtype):
    steps = 2
    count = target_columns.shape[0]
    return call(
        functools.partial(combine_kernel, gated),
        (steps,),
        [
            stepped((count // steps, TOP)),
            stepped((count // steps, TOP)),
            whole(slots.shape),
        ],
        stepped((count // steps, D)),
        jax.ShapeDtypeStruct((count, D), dtype),
    )(target_columns, gate_columns, slots)


def normalized(value):
    center = jnp.mean(value, axis=-1, keepdims=True)
    spread = jnp.mean(value * value, axis=-1, keepdims=True) - center * center
    factor = lax.rsqrt(spread + EPS)
    return (value - center) * factor, factor


def norm_back(grad, scaled, factor, gain):
    upper = grad * gain
    return factor * (
        upper
        - jnp.mean(upper, axis=-1, keepdims=True)
        - scaled * jnp.mean(upper * scaled, axis=-1, keepdims=True)
    )


def forward_kernel(
    x_ref, wq_ref, bq_ref, wp_ref, bp_ref, norm_ref, low_ref, mid_ref, tri_ref, att_ref, lse_ref
):
    x = x_ref[0].astype(F32)
    scaled, _ = normalized(x)
    low = (scaled * norm_ref[0:1, :] + norm_ref[1:2, :]).astype(BF16)
    tri = jnp.dot(low, wq_ref[...], preferred_element_type=F32) + bq_ref[...]
    tri_ref[0] = tri.astype(BF16)
    lane = lax.broadcasted_iota(jnp.int32, (PAD, PAIR), 1)
    shut = lax.broadcasted_iota(jnp.int32, (PAD, PAD), 1) >= SEQ
    logs = jnp.zeros((PAD, 128), F32)
    column = lax.broadcasted_iota(jnp.int32, (PAD, 128), 1)
    for pair in range(HEADS // 2):
        at = pair * PAIR
        query = tri_ref[0, :, at : at + PAIR]
        keys = tri_ref[0, :, D + at : D + at + PAIR]
        values = tri_ref[0, :, 2 * D + at : 2 * D + at + PAIR]
        outs = []
        for side in range(2):
            mine = (lane // HEAD_DIM) == side
            scores = contract(jnp.where(mine, query, jnp.zeros_like(query)), keys, 1, 1) * SCALE
            scores = jnp.where(shut, FAR, scores)
            peak = jnp.max(scores, axis=-1, keepdims=True)
            expo = jnp.exp(scores - peak)
            total = jnp.sum(expo, axis=-1, keepdims=True)
            prob = (expo / total).astype(BF16)
            outs.append(jnp.dot(prob, values, preferred_element_type=F32))
            logs = jnp.where(column == 2 * pair + side, peak + jnp.log(total), logs)
        att_ref[0, :, at : at + PAIR] = jnp.where(lane < HEAD_DIM, outs[0], outs[1]).astype(BF16)
    lse_ref[0] = logs
    branch = jnp.dot(att_ref[0], wp_ref[...], preferred_element_type=F32) + bp_ref[...]
    middle = x + branch
    mid_ref[0] = middle
    scaled2, _ = normalized(middle)
    low_ref[0] = (scaled2 * norm_ref[2:3, :] + norm_ref[3:4, :]).astype(BF16)


def attention_forward(x, wq, bq, wp, bp, norms):
    images = x.shape[0]
    return call(
        forward_kernel,
        (images,),
        [
            stepped((1, PAD, D)),
            whole(wq.shape),
            whole(bq.shape),
            whole(wp.shape),
            whole(bp.shape),
            whole(norms.shape),
        ],
        [
            stepped((1, PAD, D)),
            stepped((1, PAD, D)),
            stepped((1, PAD, 3 * D)),
            stepped((1, PAD, D)),
            stepped((1, PAD, 128)),
        ],
        [
            jax.ShapeDtypeStruct((images, PAD, D), BF16),
            jax.ShapeDtypeStruct((images, PAD, D), F32),
            jax.ShapeDtypeStruct((images, PAD, 3 * D), BF16),
            jax.ShapeDtypeStruct((images, PAD, D), BF16),
            jax.ShapeDtypeStruct((images, PAD, 128), F32),
        ],
    )(x, wq, bq, wp, bp, norms)


def backward_kernel(
    x_ref,
    mid_ref,
    cot_ref,
    own_ref,
    got_ref,
    tri_ref,
    att_ref,
    lse_ref,
    wq_ref,
    wp_ref,
    norm_ref,
    grad_ref,
    dwq_ref,
    dwp_ref,
    sums_ref,
    tg_ref,
):
    @pl.when(pl.program_id(0) == 0)
    def _():
        dwq_ref[...] = jnp.zeros_like(dwq_ref)
        dwp_ref[...] = jnp.zeros_like(dwp_ref)
        sums_ref[...] = jnp.zeros_like(sums_ref)

    low_grad = own_ref[0] + got_ref[0].astype(F32)
    scaled2, factor2 = normalized(mid_ref[0])
    sums_ref[2:3, :] += jnp.sum(low_grad * scaled2, axis=0, keepdims=True)
    sums_ref[3:4, :] += jnp.sum(low_grad, axis=0, keepdims=True)
    mid_grad = cot_ref[0].astype(F32) + norm_back(low_grad, scaled2, factor2, norm_ref[2:3, :])
    branch = mid_grad.astype(BF16)
    sums_ref[4:5, :] += jnp.sum(branch.astype(F32), axis=0, keepdims=True)
    dwp_ref[...] += contract(att_ref[0], branch, 0, 0)
    att_grad = contract(branch, wp_ref[...], 1, 1).astype(BF16)
    lane = lax.broadcasted_iota(jnp.int32, (PAD, PAIR), 1)
    shut = lax.broadcasted_iota(jnp.int32, (PAD, PAD), 1) >= SEQ
    for pair in range(HEADS // 2):
        at = pair * PAIR
        query = tri_ref[0, :, at : at + PAIR]
        keys = tri_ref[0, :, D + at : D + at + PAIR]
        values = tri_ref[0, :, 2 * D + at : 2 * D + at + PAIR]
        upstream = att_grad[:, at : at + PAIR]
        query_grads = []
        key_grad = jnp.zeros((PAD, PAIR), F32)
        value_grad = jnp.zeros((PAD, PAIR), F32)
        for side in range(2):
            mine = (lane // HEAD_DIM) == side
            query_one = jnp.where(mine, query, jnp.zeros_like(query))
            grad_one = jnp.where(mine, upstream, jnp.zeros_like(upstream))
            scores = contract(query_one, keys, 1, 1) * SCALE
            scores = jnp.where(shut, FAR, scores)
            head = 2 * pair + side
            prob = jnp.exp(scores - lse_ref[0, :, head : head + 1])
            prob_grad = contract(grad_one, values, 1, 1)
            value_grad += contract(prob.astype(BF16), grad_one, 0, 0)
            inside = jnp.sum(prob * prob_grad, axis=-1, keepdims=True)
            score_grad = (prob * (prob_grad - inside)).astype(BF16)
            query_grads.append(jnp.dot(score_grad, keys, preferred_element_type=F32))
            key_grad += contract(score_grad, query_one, 0, 0)
        query_grad = jnp.where(lane < HEAD_DIM, query_grads[0], query_grads[1])
        tg_ref[:, at : at + PAIR] = (query_grad * SCALE).astype(BF16)
        tg_ref[:, D + at : D + at + PAIR] = (key_grad * SCALE).astype(BF16)
        tg_ref[:, 2 * D + at : 2 * D + at + PAIR] = value_grad.astype(BF16)
    tri_grad = tg_ref[...]
    sums_ref[5:6, :] += jnp.sum(tri_grad[:, :D].astype(F32), axis=0, keepdims=True)
    sums_ref[6:7, :] += jnp.sum(tri_grad[:, 2 * D :].astype(F32), axis=0, keepdims=True)
    scaled, factor = normalized(x_ref[0].astype(F32))
    low = (scaled * norm_ref[0:1, :] + norm_ref[1:2, :]).astype(BF16)
    dwq_ref[...] += contract(low, tri_grad, 0, 0)
    normed_grad = contract(tri_grad, wq_ref[...], 1, 1)
    sums_ref[0:1, :] += jnp.sum(normed_grad * scaled, axis=0, keepdims=True)
    sums_ref[1:2, :] += jnp.sum(normed_grad, axis=0, keepdims=True)
    grad_ref[0] = (mid_grad + norm_back(normed_grad, scaled, factor, norm_ref[0:1, :])).astype(BF16)


def attention_backward(x, middle, cot, own, got, tri, att, lse, wq, wp, norms):
    images = x.shape[0]
    return call(
        backward_kernel,
        (images,),
        [
            stepped((1, PAD, D)),
            stepped((1, PAD, D)),
            stepped((1, PAD, D)),
            stepped((1, PAD, D)),
            stepped((1, PAD, D)),
            stepped((1, PAD, 3 * D)),
            stepped((1, PAD, D)),
            stepped((1, PAD, 128)),
            whole(wq.shape),
            whole(wp.shape),
            whole(norms.shape),
        ],
        [
            stepped((1, PAD, D)),
            whole((D, 3 * D)),
            whole((D, D)),
            whole((8, D)),
        ],
        [
            jax.ShapeDtypeStruct((images, PAD, D), BF16),
            jax.ShapeDtypeStruct((D, 3 * D), F32),
            jax.ShapeDtypeStruct((D, D), F32),
            jax.ShapeDtypeStruct((8, D), F32),
        ],
        scratch=[pltpu.VMEM((PAD, 3 * D), BF16)],
    )(x, middle, cot, own, got, tri, att, lse, wq, wp, norms)


STEPS = 4


def active_grad_kernel(grad_ref, wc_ref, out_ref):
    features, hidden = wc_ref.shape[3], wc_ref.shape[2]
    left, right = grad_ref[:, :features], grad_ref[:, features:]
    for half in range(2):
        part = contract(left, wc_ref[0, half], 1, 1) + contract(right, wc_ref[1, half], 1, 1)
        out_ref[:, half * hidden : (half + 1) * hidden] = part.astype(BF16)


def expert_kernel(
    slots_ref, gact_ref, we_ref, be_ref, act_ref, inner_grad_ref, slot_grad_ref, bias_grad_ref
):
    @pl.when(pl.program_id(0) == 0)
    def _():
        bias_grad_ref[...] = jnp.zeros_like(bias_grad_ref)

    features, hidden = we_ref.shape[2], we_ref.shape[3]
    left, right = slots_ref[:, :features], slots_ref[:, features:]
    chunk = hidden // 2
    grads = [None, None]
    for half in range(2):
        for piece in range(2):
            lo = piece * chunk
            at = half * hidden + lo
            inner = (
                jnp.dot(left, we_ref[0, half, :, lo : lo + chunk], preferred_element_type=F32)
                + jnp.dot(right, we_ref[1, half, :, lo : lo + chunk], preferred_element_type=F32)
                + be_ref[:, at : at + chunk]
            )
            share = 0.5 * (1.0 + lax.erf(inner * ROOT_HALF))
            act_ref[:, at : at + chunk] = (inner * share).astype(BF16)
            slope = share + inner * (DENSITY * jnp.exp(-0.5 * inner * inner))
            grad = (gact_ref[:, at : at + chunk].astype(F32) * slope).astype(BF16)
            inner_grad_ref[:, at : at + chunk] = grad
            bias_grad_ref[:, at : at + chunk] += jnp.sum(
                grad.astype(F32), axis=0, keepdims=True
            )
            for side in range(2):
                term = contract(grad, we_ref[side, half, :, lo : lo + chunk], 1, 1)
                grads[side] = term if grads[side] is None else grads[side] + term
    for side in range(2):
        slot_grad_ref[:, side * features : (side + 1) * features] = grads[side].astype(BF16)


def outer_kernel(act_ref, wc_ref, bc_ref, out_ref):
    features, hidden = wc_ref.shape[3], wc_ref.shape[2]
    for side in range(2):
        at = side * features
        total = (
            jnp.dot(act_ref[:, :hidden], wc_ref[side, 0], preferred_element_type=F32)
            + jnp.dot(act_ref[:, hidden:], wc_ref[side, 1], preferred_element_type=F32)
            + bc_ref[:, at : at + features]
        )
        out_ref[:, at : at + features] = total.astype(BF16)


def contract_grad_kernel(act_ref, grad_ref, out_ref, bias_ref):
    features = out_ref.shape[3]
    product = contract(act_ref[...], grad_ref[...], 0, 0)
    for side in range(2):
        out_ref[side, 0] = product[:, side * features : (side + 1) * features].astype(BF16)

    @pl.when(pl.program_id(0) == 0)
    def _():
        bias_ref[...] = jnp.sum(grad_ref[...].astype(F32), axis=0, keepdims=True)


def expand_grad_kernel(slots_ref, grad_ref, out_ref):
    features = out_ref.shape[2]
    product = contract(slots_ref[...], grad_ref[...], 0, 0)
    for side in range(2):
        out_ref[side, 0] = product[side * features : (side + 1) * features, :].astype(BF16)


def active_grad(grad_slots, wc):
    rows, hidden = grad_slots.shape[0], 2 * wc.shape[2]
    return call(
        active_grad_kernel,
        (STEPS,),
        [stepped((rows // STEPS, D)), whole(wc.shape)],
        stepped((rows // STEPS, hidden)),
        jax.ShapeDtypeStruct((rows, hidden), BF16),
    )(grad_slots, wc)


def experts_middle(slots, gact, we, be):
    rows, hidden = gact.shape
    return call(
        expert_kernel,
        (STEPS,),
        [
            stepped((rows // STEPS, D)),
            stepped((rows // STEPS, hidden)),
            whole(we.shape),
            whole(be.shape),
        ],
        [
            stepped((rows // STEPS, hidden)),
            stepped((rows // STEPS, hidden)),
            stepped((rows // STEPS, D)),
            whole((1, hidden)),
        ],
        [
            jax.ShapeDtypeStruct((rows, hidden), BF16),
            jax.ShapeDtypeStruct((rows, hidden), BF16),
            jax.ShapeDtypeStruct((rows, D), BF16),
            jax.ShapeDtypeStruct((1, hidden), F32),
        ],
    )(slots, gact, we, be)


def experts_outer(act, wc, bc):
    rows, hidden = act.shape
    return call(
        outer_kernel,
        (STEPS,),
        [stepped((rows // STEPS, hidden)), whole(wc.shape), whole(bc.shape)],
        stepped((rows // STEPS, D)),
        jax.ShapeDtypeStruct((rows, D), BF16),
    )(act, wc, bc)


def contract_grad(act, grad_slots):
    rows, hidden = act.shape
    chunk = hidden // STEPS
    return call(
        contract_grad_kernel,
        (STEPS,),
        [stepped((rows, chunk), 1), whole(grad_slots.shape)],
        [
            pl.BlockSpec((2, 1, chunk, D // 2), lambda g: (0, g // 2, g % 2, 0)),
            whole((1, D)),
        ],
        [
            jax.ShapeDtypeStruct((2, 2, hidden // 2, D // 2), BF16),
            jax.ShapeDtypeStruct((1, D), F32),
        ],
    )(act, grad_slots)


def expand_grad(slots, inner_grad):
    rows, hidden = inner_grad.shape
    chunk = hidden // STEPS
    return call(
        expand_grad_kernel,
        (STEPS,),
        [whole(slots.shape), stepped((rows, chunk), 1)],
        pl.BlockSpec((2, 1, D // 2, chunk), lambda g: (0, g // 2, 0, g % 2)),
        jax.ShapeDtypeStruct((2, 2, D // 2, hidden // 2), BF16),
    )(slots, inner_grad)


def expert_weight(block, row, col):
    if block.shape[0] == 1:
        halves = in_order(col, block, swap(block, "col"), 0)
    else:
        split = block.reshape((2, 2) + block.shape[1:])
        got = swap(chosen(split, 1 - col, 1), "col")
        kept = chosen(split, col, 1)
        halves = in_order(col, kept[:, None], got[:, None], 1)
    if block.shape[0] == 1:
        return in_order(row, halves[None], swap(halves, "row")[None], 0)
    got = swap(chosen(halves, 1 - row), "row")
    return in_order(row, chosen(halves, row)[None], got[None], 0)


def expert_weight_grad(grad, row, col, experts):
    got = swap(chosen(grad, 1 - row), "row")
    kept = chosen(grad, row)
    if experts == 1:
        halves = (kept.astype(F32) + got.astype(F32)).astype(BF16)
        got = swap(chosen(halves, 1 - col), "col")
        return (chosen(halves, col).astype(F32) + got.astype(F32))[None]
    both = in_order(row, kept[None], got[None], 0)
    got = swap(chosen(both, 1 - col, 1), "col")
    kept = chosen(both, col, 1)
    return in_order(col, kept[:, None], got[:, None], 1).reshape((4,) + grad.shape[2:]).astype(F32)


def bits_of(size):
    bits = []
    bit = size // 2
    order = []
    while bit:
        order.append(bit)
        bit //= 2
    bits = order[1::-1] + order[2:] if len(order) > 2 else order
    return bits


def gathered(block, size):
    order = []
    bit = size // 2
    while bit:
        order.append(bit)
        bit //= 2
    held = block.reshape((1,) * (len(order) + 2) + block.shape)
    place = lax.axis_index("dp")
    for bit in bits_of(size):
        axis = order.index(bit)
        held = in_order((place // bit) % 2, held, swap(held, "dp", bit), axis)
    held = in_order(lax.axis_index("col"), held, swap(held, "col"), len(order))
    held = in_order(lax.axis_index("row"), held, swap(held, "row"), len(order) + 1)
    return held.reshape((size, 2, 2) + block.shape)


def summed(blocks, size):
    order = []
    bit = size // 2
    while bit:
        order.append(bit)
        bit //= 2
    held = blocks.reshape((2,) * (len(order) + 2) + blocks.shape[3:])

    def halve(held, axis_name, bit, index, axis):
        got = swap(lax.dynamic_slice_in_dim(held, 1 - index, 1, axis), axis_name, bit)
        kept = lax.dynamic_slice_in_dim(held, index, 1, axis)
        return kept.astype(F32) + got.astype(F32)

    held = halve(held, "row", 1, lax.axis_index("row"), len(order) + 1).astype(BF16)
    held = halve(held, "col", 1, lax.axis_index("col"), len(order)).astype(BF16)
    place = lax.axis_index("dp")
    bits = bits_of(size)[::-1]
    for bit in bits:
        held = halve(held, "dp", bit, (place // bit) % 2, order.index(bit))
        held = held if bit == bits[-1] else held.astype(BF16)
    return held.reshape(blocks.shape[3:])


def everywhere(value, size):
    value = value + swap(value, "row")
    value = value + swap(value, "col")
    for bit in bits_of(size)[::-1]:
        value = value + swap(value, "dp", bit)
    return value


def as_rows(value, width):
    flat = value.reshape(-1)
    return jnp.pad(flat, (0, round_up(flat.shape[0], width) - flat.shape[0])).reshape(-1, width)


def on_device(
    tokens_in,
    out_cotangent,
    expert_ids,
    gate_values,
    first_gain,
    first_shift,
    second_gain,
    second_shift,
    qkv_weight,
    qkv_bias,
    proj_weight,
    proj_bias,
    expand_weight,
    expand_bias,
    contract_weight,
    contract_bias,
):
    size = lax.axis_size("dp")
    row, col, place = lax.axis_index("row"), lax.axis_index("col"), lax.axis_index("dp")
    local_rows, width = tokens_in.shape[1:]
    group = expert_ids.shape[1]
    images = local_rows // SEQ
    capacity = (group * TOP * 4 + 3 * EXPERTS - 1) // (3 * EXPERTS)
    local_experts = EXPERTS // size
    share = local_experts * capacity // 4
    held_rows = round_up(share, 8)
    peers = 2 * size
    rows = peers * held_rows

    block = jnp.concatenate(
        [
            as_rows(qkv_weight.transpose(1, 0, 2), width),
            as_rows(proj_weight, width),
            as_rows(expand_bias.astype(BF16), width),
            as_rows(contract_bias.astype(BF16), width),
            as_rows(qkv_bias.astype(BF16), width),
            as_rows(proj_bias.astype(BF16), width),
        ],
        0,
    )
    block = jnp.pad(block, ((0, round_up(block.shape[0], 16) - block.shape[0]), (0, 0)))
    parts = gathered(block, size)

    def taken(start, like):
        count = like.size // width if like.size >= width else 1
        found = parts[:, :, :, start : start + count]
        flat = found.reshape(found.shape[:3] + (-1,))[..., : like.size]
        return flat.reshape(found.shape[:3] + like.shape), start + count

    depth = qkv_weight.shape[0]
    wq, at = taken(0, qkv_weight.transpose(1, 0, 2))
    wq = wq.transpose(2, 0, 4, 3, 1, 5).reshape(D, 3 * D)
    wp, at = taken(at, proj_weight)
    wp = wp.transpose(1, 0, 3, 2, 4).reshape(D, D)
    be, at = taken(at, expand_bias)
    expert = place * local_experts + (2 * row + col) * local_experts // 4
    be = chosen(be, expert // (EXPERTS // 2), 2)
    be = chosen(be, expert % (EXPERTS // 2), 2)
    be = be.transpose(1, 0, 2).reshape(1, -1).astype(F32)
    bc, at = taken(at, contract_bias)
    bc = chosen(bc[:, 0], expert, 2).transpose(1, 0, 2).reshape(1, D).astype(F32)
    bq, at = taken(at, qkv_bias)
    bq = bq[:, :, 0].transpose(2, 1, 0, 3).reshape(2, D).astype(F32)
    bq = jnp.concatenate([bq[0], jnp.zeros((D,), F32), bq[1]]).reshape(1, 3 * D)
    bp, at = taken(at, proj_bias)
    bp = bp[:, 0].transpose(1, 0, 2).reshape(1, D).astype(F32)
    norms = jnp.stack([first_gain, first_shift, second_gain, second_shift])
    norms = in_order(row, norms, swap(norms, "row"), 1)

    def by_image(array):
        shaped = array.reshape(2, images, SEQ, width)
        return jnp.pad(shaped, ((0, 0), (0, 0), (0, PAD - SEQ), (0, 0)))

    same = row == col

    def to_chip(array):
        own = chosen(array, col)
        got = swap(chosen(array, 1 - col), "col")
        return either(same, own, got), either(same, got, own)

    kept, sent = to_chip(by_image(tokens_in))
    x = in_order(row, kept, swap(sent, "row"), 2)
    kept, sent = to_chip(by_image(out_cotangent))
    cot = in_order(
        row, jnp.stack([kept, sent]), swap(jnp.stack([sent, kept]), "row"), 3
    )

    routes = chosen(expert_ids, col)
    gates = chosen(gate_values, col)
    slot = destinations(routes, capacity)
    unit = routes % local_experts * capacity + slot
    home = unit // share
    target = (routes // local_experts * 2 + home % 2) * held_rows + unit % share
    target = jnp.where(home // 2 == row, target, -1)

    def own_first(array, fill):
        shaped = array.reshape(2, images, SEQ, TOP)
        shaped = jnp.pad(
            shaped, ((0, 0), (0, 0), (0, PAD - SEQ), (0, 0)), constant_values=fill
        ).reshape(2, images * PAD, TOP)
        return jnp.where(row == 0, shaped, shaped[::-1])

    target = own_first(target, -1)
    gates = own_first(gates, 0)
    target_rows = target.transpose(0, 2, 1).reshape(2 * TOP, images * PAD)
    gate_rows = gates.transpose(0, 2, 1).reshape(2 * TOP, images * PAD)

    def exchange(slots):
        shaped = slots.reshape(peers, held_rows, D)
        return lax.all_to_all(shaped, ("dp", "col"), 0, 0, tiled=True).reshape(rows, D)

    def flat(array):
        return array.reshape(images * PAD, D)

    grad_slots = dispatch(target_rows, gate_rows, flat(cot[0]), flat(cot[1]), rows, True)
    grad_slots = exchange(grad_slots)
    we = expert_weight(expand_weight, row, col)
    wc = expert_weight(contract_weight, row, col)
    gact = active_grad(grad_slots, wc)

    low, middle, tri, att, lse = attention_forward(x, wq, bq, wp, bp, norms)
    low = flat(low)
    slots = dispatch(target_rows, gate_rows, low, swap(low, "row"), rows, False)
    slots = exchange(slots)
    act, inner_grad, slot_grad, be_grad = experts_middle(slots, gact, we, be)
    slot_grad = exchange(slot_grad)
    outer = exchange(experts_outer(act, wc, bc))
    wc_grad, bc_grad = contract_grad(act, grad_slots)
    we_grad = expand_grad(slots, inner_grad)
    we_grad = expert_weight_grad(we_grad, row, col, local_experts)
    wc_grad = expert_weight_grad(wc_grad, row, col, local_experts)

    def back(array, gated):
        sent = combine(target[1], gates[1], array, gated, BF16)
        got = swap(sent, "row")
        own = combine(target[0], gates[0], array, gated, F32)
        return own, got

    def to_image(array):
        return array.reshape(images, PAD, D)

    own, got = back(slot_grad, False)
    x_grad, wq_grad, wp_grad, sums = attention_backward(
        x, middle, cot[0], to_image(own), to_image(got), tri, att, lse, wq, wp, norms
    )
    own, got = back(outer, True)
    layer_out = (flat(middle) + own + got.astype(F32)).astype(BF16)

    def to_tokens(array):
        shaped = array.reshape(images, PAD, 2, width)[:, :SEQ].reshape(local_rows, 2, width)
        kept = chosen(shaped, row, 1)
        got = swap(chosen(shaped, 1 - row, 1), "row")
        own, other = either(same, kept, got), either(same, got, kept)
        return in_order(col, own[None], swap(other, "col")[None], 0)

    piece = wq_grad.reshape(2, size, depth, 3, 2, width).transpose(1, 4, 0, 3, 2, 5)
    pieces = [piece.astype(BF16)]
    pieces.append(wp_grad.reshape(2, size, -1, 2, width).transpose(1, 0, 3, 2, 4).astype(BF16))
    hidden_part = expand_bias.shape[1]
    mine = (jnp.arange(EXPERTS, dtype=jnp.int32) == expert).astype(F32)
    piece = mine.reshape(1, 1, 2, EXPERTS // 2, 1) * be_grad.reshape(
        2, size, hidden_part
    ).transpose(1, 0, 2).reshape(size, 2, 1, 1, hidden_part)
    pieces.append(piece.astype(BF16))
    feature_part = contract_bias.shape[1]
    piece = mine.reshape(1, 1, EXPERTS, 1) * bc_grad.reshape(2, size, feature_part).transpose(
        1, 0, 2
    ).reshape(size, 2, 1, feature_part)
    pieces.append(jnp.broadcast_to(piece[:, None], (size, 2) + piece.shape[1:]).astype(BF16))
    bias_grads = sums[5:7].reshape(2, 2, size, -1).transpose(2, 1, 0, 3)
    pieces.append(
        jnp.broadcast_to(bias_grads[:, :, None], (size, 2, 2) + bias_grads.shape[2:]).astype(BF16)
    )
    proj_grads = sums[4].reshape(2, size, -1).transpose(1, 0, 2)
    pieces.append(
        jnp.broadcast_to(proj_grads[:, None], (size, 2) + proj_grads.shape[1:]).astype(BF16)
    )

    def as_blocks(piece):
        shaped = piece.reshape(size, 2, 2, -1)
        count = shaped.shape[-1]
        shaped = jnp.pad(shaped, ((0, 0),) * 3 + ((0, round_up(count, width) - count),))
        return shaped.reshape(size, 2, 2, -1, width)

    blocks = jnp.concatenate([as_blocks(piece) for piece in pieces], 3)
    short = round_up(blocks.shape[3], 16) - blocks.shape[3]
    blocks = jnp.pad(blocks, ((0, 0),) * 3 + ((0, short), (0, 0)))
    reduced = summed(blocks, size)

    def given(start, like):
        count = like.size // width if like.size >= width else 1
        found = reduced[start : start + count].reshape(-1)[: like.size]
        return found.reshape(like.shape), start + count

    out_wq, at = given(0, qkv_weight.transpose(1, 0, 2))
    out_wq = out_wq.transpose(1, 0, 2)
    out_wp, at = given(at, proj_weight)
    out_be, at = given(at, expand_bias)
    out_bc, at = given(at, contract_bias)
    out_bq, at = given(at, qkv_bias)
    out_bp, at = given(at, proj_bias)
    norm_total = everywhere(sums[:4], size)
    norm_total = lax.dynamic_slice_in_dim(norm_total, row * width, width, 1)
    return (
        to_tokens(layer_out),
        to_tokens(x_grad).astype(F32),
        norm_total[0],
        norm_total[1],
        norm_total[2],
        norm_total[3],
        out_wq,
        out_bq,
        out_wp,
        out_bp,
        we_grad,
        out_be,
        wc_grad,
        out_bc,
    )


def solution(mesh):
    return jax.shard_map(
        on_device,
        mesh=mesh,
        in_specs=(
            P(None, ("dp", "col"), "row"),
            P(None, ("dp", "col"), "row"),
            P(None, "dp", None),
            P(None, "dp", None),
            P("row"),
            P("row"),
            P("row"),
            P("row"),
            P(("row", "dp"), None, "col"),
            P(None, ("col", "dp")),
            P(("col", "dp"), "row"),
            P(("row", "dp")),
            P("dp", "row", "col"),
            P("row", ("col", "dp")),
            P("dp", "col", "row"),
            P(None, ("row", "dp")),
        ),
        out_specs=(
            P(None, ("dp", "col"), "row"),
            P(None, ("dp", "col"), "row"),
            P("row"),
            P("row"),
            P("row"),
            P("row"),
            P(("row", "dp"), None, "col"),
            P(None, ("col", "dp")),
            P(("col", "dp"), "row"),
            P(("row", "dp")),
            P("dp", "row", "col"),
            P("row", ("col", "dp")),
            P("dp", "col", "row"),
            P(None, ("row", "dp")),
        ),
        check_vma=False,
    )
```

time: 1960 us -> 500 us (0.26)
  waiting for transfers between devices: 633 us -> 156 us
  blocking collectives: 431 us -> 0 us
  matrix products: 277 us -> 1.03 us
  local copies, waits for them, and re-layouts: 331 us -> 98.9 us
  other arithmetic: 227 us -> 61.9 us
  Pallas kernels: 0 us -> 111 us
  starting transfers between devices: 24.3 us -> 63.7 us
  between operations: 21.7 us -> 1.94 us
    reduce_scatter x8 -> x0, waiting for transfers between devices: 478 us -> none  [the longest x1 279 us: on_device(): lax.psum_scatter(sums[6].astype(jnp.bfloat16), 'dp', scatter_dimension=0,...]
    dot_general x40 -> x1, matrix products: 277 us -> 1.03 us  [destinations(): jnp.dot(earlier, named.sum(axis=1).astype(BF16), preferred_element_type=F32)]
    all_gather x15 -> x0, blocking collectives: 255 us -> none  [the longest x4 63.3 us: grad_rows(): return lax.all_gather(value, 'col', axis=0, tiled=True)]
    all_gather x8 -> x0, waiting for transfers between devices: 153 us -> none  [the longest x1 143 us: fetch_blocks(): lax.all_gather(contract_weight, 'dp', axis=0, tiled=True)]
    unnamed x6 -> x0, blocking collectives: 123 us -> none
    ppermute x0 -> x35, waiting for transfers between devices: none -> 120 us  [swap(): lax.ppermute(value, axis, [(place, place ^ bit) for place in range(size)])]
    reduce_sum x22 -> x2, other arithmetic: 111 us -> 0.13 us  [the longest x1 0.08 us: destinations(): return jnp.sum(before[:, None, :] * named, axis=2).astype(jnp.int32)]
    pallas_call x0 -> x13, Pallas kernels: none -> 111 us  [the longest x1 20.9 us: attention_backward(): call(backward_kernel, (images,), [stepped((1, PAD, D)), stepped((1, PAD,...]
  transfers between devices with their start and end apart: 30 -> 39, of which waited for: 7 -> 14; matrix products, arithmetic and copies ran while one was open for 37% -> 27% of each run, Pallas kernels for 0% -> 18%
where the time goes in v1:
time: 500 us; the launch traced here: 494 us
  waiting for transfers between devices  156 us (31%)
  Pallas kernels  111 us (22%)
  local copies, waits for them, and re-layouts  98.9 us (20%)
  starting transfers between devices  63.7 us (13%)
  other arithmetic  61.9 us (12%)
    ppermute x35, waiting for transfers between devices, swap(): lax.ppermute(value, axis, [(place, place ^ bit) for place in range(size)])  120 us
    all_to_all x4, waiting for transfers between devices, exchange(): lax.all_to_all(shaped, ('dp', 'col'), 0, 0, tiled=True).reshape(rows, D)  35.9 us
    all_to_all x4, starting transfers between devices, exchange(): lax.all_to_all(shaped, ('dp', 'col'), 0, 0, tiled=True).reshape(rows, D)  33.8 us
    select_n x20, other arithmetic, in_order(): jnp.where(index == 0, jnp.concatenate([own, other], axis), jnp.concatenat...  33.3 us
    ppermute x35, starting transfers between devices, swap(): lax.ppermute(value, axis, [(place, place ^ bit) for place in range(size)])  29.9 us
    unnamed x100, local copies, waits for them, and re-layouts  23.9 us
    pallas_call x1, Pallas kernels, attention_backward(): call(backward_kernel, (images,), [stepped((1, PAD, D)), stepped((1, PAD,...  20.9 us
    pallas_call x1, Pallas kernels, experts_middle(): call(expert_kernel, (STEPS,), [stepped((rows // STEPS, D)), stepped((rows...  20.5 us
  transfers between devices with their start and end apart: 39, of which 14 were waited for; matrix products, arithmetic and copies ran while one was open for 27% of the time, Pallas kernels for 18%

profile of v1, /device:TPU:0, one launch (start us, length us, event | category | flops | bytes accessed | tf_op | source)
XLA Modules:
  0.0 493.9 jit_solution(11530094235543251183)
XLA Ops:
  5.3 3.1 collective-permute-start.2
  17.8 2.6 collective-permute-start.3
  20.4 10.6 %collective-permute-done.9 = bf16[4,208,256]{2,1,0:T(8,128)(2,1)S(1)} collective-permute-done((bf16[4,208,256]{2,1,0:T(8,128)(2,1)}, bf16[4,208,256]{2,1,0:T(8,128)(2,1)S(1)}, u32[]{:S(2)}, u32[]{:S(2)}) %collective-permute-start.9) | collective-permute-done | bytes 426016 | tf_op jit(solution)/shard_map/ppermute | solution.py:37
  34.8 1.8 copy.138
  42.1 1.9 fusion.34
  44.0 3.8 collective-permute-done.4
  50.1 1.9 maximum_select_fusion.9
  53.2 5.3 %shard_map.265 = bf16[2176,512]{1,0:T(8,128)(2,1)S(1)} custom-call(s32[4,832]{1,0:T(4,128)S(1)} %reshape.1107.target_ref, f32[4,832]{1,0:T(4,128)S(1)} %reshape.1108.gate_ref, bf16[832,512]{1,0:T(8,128)(2,1)S(1)} %bitcast.258, bf16[832,512]{1,0:T(8,128)(2,1)S(1)} %bitcast.257), custom_call_target="tpu_custom_call" | custom-call | tf_op jit(solution)/shard_map/pallas_call | solution.py:119
  59.9 5.5 %all-to-all-start.1 = ((bf16[16,136,512]{2,1,0:T(8,128)(2,1)}), bf16[16,136,512]{2,1,0:T(8,128)(2,1)S(1)}, u32[]{:S(2)}, u32[]{:S(2)}) async-start(bf16[16,136,512]{2,1,0:T(8,128)(2,1)} %bitcast.253), calls=%async_computation.1 | async-start | bytes 4456448 | tf_op jit(solution)/shard_map/all_to_all | solution.py:702
  77.6 4.2 copy.189
  81.8 4.8 reshape.1097.wq_ref
  88.5 9.0 %shard_map.263 = (bf16[4,208,512]{2,1,0:T(8,128)(2,1)S(1)}, f32[4,208,512]{2,1,0:T(8,128)}, bf16[4,208,1536]{2,1,0:T(8,128)(2,1)}, bf16[4,208,512]{2,1,0:T(8,128)(2,1)S(1)}, f32[4,208,128]{2,1,0:T(8,128)S(1)}) custom-call(bf16[4,208,512]{2,1,0:T(8,128)(2,1)S(1)} %maximum_select_fusion.12.x_ref, bf16[512,1536]{1,0:T(8,128)(2,1)S(1)} %copy-done.4, ...), custom_call_target="tpu_custom_call" | custom-call | tf_op jit(solution)/shard_map/pallas_call | solution.py:212
  99.3 2.2 collective-permute-done.8.other_ref
  101.5 5.3 %shard_map.264 = bf16[2176,512]{1,0:T(8,128)(2,1)S(1)} custom-call(s32[4,832]{1,0:T(4,128)S(1)} %reshape.1107.target_ref, f32[4,832]{1,0:T(4,128)S(1)} %reshape.1108.gate_ref, bf16[832,512]{1,0:T(8,128)(2,1)S(1)} %bitcast.261, bf16[832,512]{1,0:T(8,128)(2,1)S(1)} %collective-permute-done.8.other_ref), custom_call_target="tpu_custom_call" | custom-call | tf_op jit(solution)/shard_map/pallas_call | solution.py:119
  108.2 2.2 all-to-all-done.1
  110.4 10.5 %all-to-all-start = ((bf16[16,136,512]{2,1,0:T(8,128)(2,1)}), bf16[16,136,512]{2,1,0:T(8,128)(2,1)}, u32[]{:S(2)}, u32[]{:S(2)}) async-start(bf16[16,136,512]{2,1,0:T(8,128)(2,1)} %bitcast.252), calls=%async_computation | async-start | bytes 4456448 | tf_op jit(solution)/shard_map/all_to_all | solution.py:702
  121.0 3.2 constant_dynamic-slice_fusion.18
  124.2 2.0 collective-permute-start.13
  127.7 43.5 %collective-permute-done.13 = bf16[2,256,1024]{2,1,0:T(8,128)(2,1)} collective-permute-done((bf16[2,256,1024]{2,1,0:T(8,128)(2,1)}, bf16[2,256,1024]{2,1,0:T(8,128)(2,1)}, u32[]{:S(2)}, u32[]{:S(2)}) %collective-permute-start.13) | collective-permute-done | bytes 1048608 | tf_op jit(solution)/shard_map/ppermute | solution.py:37
  171.1 2.6 maximum_select_fusion.3
  175.2 16.2 %collective-permute-done.11 = bf16[2,1024,256]{2,1,0:T(8,128)(2,1)} collective-permute-done((bf16[2,1024,256]{2,1,0:T(8,128)(2,1)}, bf16[2,1024,256]{2,1,0:T(8,128)(2,1)}, u32[]{:S(2)}, u32[]{:S(2)}) %collective-permute-start.11) | collective-permute-done | bytes 1048608 | tf_op jit(solution)/shard_map/ppermute | solution.py:37
  191.4 1.9 maximum_select_fusion.1
  194.9 4.0 maximum_select_fusion.4.we_ref
  198.9 3.3 maximum_select_fusion.2.wc_ref
  203.8 6.8 %shard_map.266.gact_ref = bf16[2176,2048]{1,0:T(8,128)(2,1)} custom-call(bf16[2176,512]{1,0:T(8,128)(2,1)S(1)} %bitcast.249, bf16[2,2,1024,256]{3,2,1,0:T(8,128)(2,1)S(1)} %copy-done.2), custom_call_target="tpu_custom_call" | custom-call | tf_op jit(solution)/shard_map/pallas_call | solution.py:426
  212.2 20.5 %shard_map.267 = (bf16[2176,2048]{1,0:T(8,128)(2,1)}, bf16[2176,2048]{1,0:T(8,128)(2,1)}, bf16[2176,512]{1,0:T(8,128)(2,1)S(1)}, f32[1,2048]{1,0:T(1,128)S(1)}) custom-call(bf16[2176,512]{1,0:T(8,128)(2,1)} %bitcast.47.slots_ref, bf16[2176,2048]{1,0:T(8,128)(2,1)} %shard_map.266.gact_ref, bf16[2,2,256,1024]{3,2,1,0:T(8,128)(2,1)S(1)} %copy-done.8, ...), custom_call_target="tpu_custom_call" | custom-call | tf_op jit(solution)/shard_map/pallas_call | solution.py:437
  234.1 5.8 %all-to-all-start.3 = ((bf16[16,136,512]{2,1,0:T(8,128)(2,1)}), bf16[16,136,512]{2,1,0:T(8,128)(2,1)}, u32[]{:S(2)}, u32[]{:S(2)}) async-start(bf16[16,136,512]{2,1,0:T(8,128)(2,1)} %bitcast.259), calls=%async_computation.3 | async-start | bytes 4456448 | tf_op jit(solution)/shard_map/all_to_all | solution.py:702
  242.7 7.4 %shard_map.268 = bf16[2176,512]{1,0:T(8,128)(2,1)S(1)} custom-call(bf16[2176,2048]{1,0:T(8,128)(2,1)} %get-tuple-element.31.act_ref, bf16[2,2,1024,256]{3,2,1,0:T(8,128)(2,1)S(1)} %copy-done.3, f32[1,512]{1,0:T(1,128)S(1)} %reshape.1136.bc_ref), custom_call_target="tpu_custom_call" | custom-call | tf_op jit(solution)/shard_map/pallas_call | solution.py:463
  251.5 33.7 %all-to-all-done.3 = bf16[16,136,512]{2,1,0:T(8,128)(2,1)} async-done(((bf16[16,136,512]{2,1,0:T(8,128)(2,1)}), bf16[16,136,512]{2,1,0:T(8,128)(2,1)}, u32[]{:S(2)}, u32[]{:S(2)}) %all-to-all-start.3) | async-done | bytes 2228256 | tf_op jit(solution)/shard_map/all_to_all | solution.py:702
  285.2 12.1 %all-to-all-start.2 = ((bf16[16,136,512]{2,1,0:T(8,128)(2,1)}), bf16[16,136,512]{2,1,0:T(8,128)(2,1)}, u32[]{:S(2)}, u32[]{:S(2)}) async-start(bf16[16,136,512]{2,1,0:T(8,128)(2,1)} %bitcast.251), calls=%async_computation.2 | async-start | bytes 4456448 | tf_op jit(solution)/shard_map/all_to_all | solution.py:702
  297.3 8.1 %shard_map.274 = (bf16[2,2,1024,256]{3,2,1,0:T(8,128)(2,1)S(1)}, f32[1,512]{1,0:T(1,128)S(1)}) custom-call(bf16[2176,2048]{1,0:T(8,128)(2,1)} %get-tuple-element.31.act_ref, bf16[2176,512]{1,0:T(8,128)(2,1)S(1)} %bitcast.250), custom_call_target="tpu_custom_call" | custom-call | tf_op jit(solution)/shard_map/pallas_call | solution.py:475
  308.1 8.4 %shard_map.275 = bf16[2,2,256,1024]{3,2,1,0:T(8,128)(2,1)S(1)} custom-call(bf16[2176,512]{1,0:T(8,128)(2,1)} %bitcast.47.slots_ref, bf16[2176,2048]{1,0:T(8,128)(2,1)} %get-tuple-element.42.grad_ref), custom_call_target="tpu_custom_call" | custom-call | tf_op jit(solution)/shard_map/pallas_call | solution.py:493
  318.0 1.9 maximum_select_fusion.7
  321.5 2.0 collective-permute-start.34
  325.0 5.0 %shard_map.272 = bf16[832,512]{1,0:T(8,128)(2,1)} custom-call(s32[832,2]{1,0:T(8,128)S(1)} %get-tuple-element.133.target_ref, f32[832,2]{1,0:T(8,128)S(1)} %get-tuple-element.131.gate_ref, bf16[2176,512]{1,0:T(8,128)(2,1)} %bitcast.83.slots_ref), custom_call_target="tpu_custom_call" | custom-call | tf_op jit(solution)/shard_map/pallas_call | solution.py:144
  331.5 2.6 maximum_select_fusion.5
  335.9 22.5 %collective-permute-done.34 = bf16[2,1024,256]{2,1,0:T(8,128)(2,1)} collective-permute-done((bf16[2,1024,256]{2,1,0:T(8,128)(2,1)}, bf16[2,1024,256]{2,1,0:T(8,128)(2,1)}, u32[]{:S(2)}, u32[]{:S(2)}) %collective-permute-start.34) | collective-permute-done | bytes 1048608 | tf_op jit(solution)/shard_map/ppermute | solution.py:37
  358.4 3.3 maximum_select_fusion.8
  361.7 4.3 shard_map.271
  367.2 20.9 %shard_map.273 = (bf16[4,208,512]{2,1,0:T(8,128)(2,1)S(1)}, f32[512,1536]{1,0:T(8,128)}, f32[512,512]{1,0:T(8,128)}, f32[8,512]{1,0:T(8,128)S(1)}) custom-call(bf16[4,208,512]{2,1,0:T(8,128)(2,1)S(1)} %maximum_select_fusion.12.x_ref, f32[4,208,512]{2,1,0:T(8,128)} %get-tuple-element.29.mid_ref, bf16[4,208,512]{2,1,0:T(8,128)(2,1)S(1)} %copy-done.12, ...), custom_call_target="tpu_custom_call" | custom-call | tf_op jit(solution)/shard_map/pallas_call | solution.py:316
  390.9 3.2 convert_element_type.226
  394.2 4.9 %convert_element_type.227 = bf16[2,8,32,3,2,256]{5,4,3,2,1,0:T(2,128)(2,1)} reshape(bf16[512,1536]{1,0:T(8,128)(2,1)} %convert_element_type.226) | data formatting | bytes 3145728 | tf_op jit(solution)/shard_map/convert_element_type | solution.py:749
  399.1 2.9 copy.148
  402.1 10.2 %concatenate.439 = bf16[8,2,2,142,256]{4,3,2,1,0:T(8,128)(2,1)} concatenate(bf16[8,2,2,96,256]{4,3,2,1,0:T(8,128)(2,1)} %bitcast.274, bf16[8,2,2,32,256]{4,3,2,1,0:T(8,128)(2,1)S(1)} %bitcast.281, bf16[8,2,2,8,256]{4,3,2,1,0:T(8,128)(2,1)S(1)} %copy-done.39, bf16[8,2,2,4,256]{4,3,2,1,0:T(4,128)(2,1)S(1)} %broadcast_in_dim.83, bf16[8,2,2,1,256]{4,3,2,1,0:T(2,128)(2,1)S(1)} %copy.153, ...), dimensions={3} | concatenate | bytes 4653056 | tf_op jit(solution)/shard_map/concatenate | solution.py:777
  412.3 1.8 pad.48
  415.3 1.7 copy-done.23
  417.0 2.5 bitcast_convert_fusion
  419.6 3.2 maximum_select_fusion.6
  422.8 5.3 %shard_map.270 = bf16[832,512]{1,0:T(8,128)(2,1)} custom-call(s32[832,2]{1,0:T(8,128)S(1)} %get-tuple-element.133.target_ref, f32[832,2]{1,0:T(8,128)S(1)} %get-tuple-element.131.gate_ref, bf16[2176,512]{1,0:T(8,128)(2,1)} %bitcast.73.slots_ref), custom_call_target="tpu_custom_call" | custom-call | tf_op jit(solution)/shard_map/pallas_call | solution.py:144
  429.1 2.6 bitcast_convert_fusion.1
  431.8 4.4 shard_map.269
  438.4 2.5 constant_dynamic-slice_fusion.12
  441.9 6.5 %collective-permute-start.24 = (f32[4,512]{1,0:T(4,128)S(1)}, f32[4,512]{1,0:T(4,128)S(1)}, u32[]{:S(2)}, u32[]{:S(2)}) collective-permute-start(f32[4,512]{1,0:T(4,128)S(1)} %add.235), channel_id=1, source_target_pairs={{0,16},{4,20},{8,24},{12,28},{16,0},{20,4},{24,8},{28,12},{1,17},{... | collective-permute-start | bytes 24584 | tf_op jit(solution)/shard_map/ppermute | solution.py:37
  450.0 1.7 collective-permute-start.27
  451.7 2.6 fusion.2
  454.3 2.5 reshape.1119
  457.4 1.7 constant_dynamic-slice_fusion.14
  459.3 1.8 collective-permute-done.25
  461.6 4.0 collective-permute-done.27
  469.1 1.7 collective-permute-start.20
  471.3 4.1 collective-permute-done.28
  476.3 5.2 %collective-permute-done.20 = bf16[788,256]{1,0:T(8,128)(2,1)S(1)} collective-permute-done((bf16[788,256]{1,0:T(8,128)(2,1)S(1)}, bf16[788,256]{1,0:T(8,128)(2,1)S(1)}, u32[]{:S(2)}, u32[]{:S(2)}) %collective-permute-start.20) | collective-permute-done | bytes 403488 | tf_op jit(solution)/shard_map/ppermute | solution.py:37
  481.6 2.0 copy.156
  483.9 4.4 collective-permute-done.17
  (310 shorter events, 92.2 us)
Async XLA Ops:
  0.6 12.7 %copy-start = (s32[2,1576,2]{1,2,0:T(2,128)S(1)}, s32[2,1576,2]{1,2,0:T(2,128)}, u32[]{:S(2)}) copy-start(s32[2,1576,2]{1,2,0:T(2,128)} %param.18) | copy-start | bytes 75652
  0.7 11.3 %copy-start.38 = (bf16[2,788,256]{2,0,1:T(2,128)(2,1)S(1)}, bf16[2,788,256]{2,0,1:T(2,128)(2,1)}, u32[]{:S(2)}) copy-start(bf16[2,788,256]{2,0,1:T(2,128)(2,1)} %param.17) | copy-start | bytes 2420740
  5.3 11.9 %collective-permute-start.2 = (bf16[1,1,1,1,1,144,256]{6,5,4,3,2,1,0:T(8,128)(2,1)S(1)}, bf16[1,1,1,1,1,144,256]{6,5,4,3,2,1,0:T(8,128)(2,1)S(1)}, u32[]{:S(2)}, u32[]{:S(2)}) collective-permute-start(bf16[1,1,1,1,1,144,256]{6,5,4,3,2,1,0:T(8,128)(2,1)S(1)} %get-tuple-element.148), channel_id=1, source_target_pairs={{0,8},{4,12},{8,0},{12,4},{16,24},{20,28},{24,16},{28,20},{1,9},{5... | collective-permute-start | bytes 221192 | tf_op jit(solution)/shard_map/ppermute | solution.py:37
  9.6 3.8 copy-start.41
  10.4 59.1 %collective-permute-start = (bf16[4,208,256]{2,1,0:T(8,128)(2,1)}, bf16[4,208,256]{2,1,0:T(8,128)(2,1)}, u32[]{:S(2)}, u32[]{:S(2)}) collective-permute-start(bf16[4,208,256]{2,1,0:T(8,128)(2,1)} %fusion.8), channel_id=1, source_target_pairs={{0,1},{1,0},{2,3},{3,2},{4,5},{5,4},{6,7},{7,6},{8,9},{9,8},{10,11... | collective-permute-start | bytes 1277960 | tf_op jit(solution)/shard_map/ppermute | solution.py:37
  12.8 18.2 %collective-permute-start.9 = (bf16[4,208,256]{2,1,0:T(8,128)(2,1)}, bf16[4,208,256]{2,1,0:T(8,128)(2,1)S(1)}, u32[]{:S(2)}, u32[]{:S(2)}) collective-permute-start(bf16[4,208,256]{2,1,0:T(8,128)(2,1)} %fusion.10), channel_id=1, source_target_pairs={{0,1},{1,0},{2,3},{3,2},{4,5},{5,4},{6,7},{7,6},{8,9},{9,8},{10,11... | collective-permute-start | bytes 1277960 | tf_op jit(solution)/shard_map/ppermute | solution.py:37
  17.8 19.5 %collective-permute-start.3 = (bf16[1,2,1,1,1,144,256]{6,5,2,1,0,4,3:T(8,128)(2,1)}, bf16[1,2,1,1,1,144,256]{6,5,2,1,0,4,3:T(8,128)(2,1)S(1)}, u32[]{:S(2)}, u32[]{:S(2)}) collective-permute-start(bf16[1,2,1,1,1,144,256]{6,5,2,1,0,4,3:T(8,128)(2,1)} %fusion.12), channel_id=1, source_target_pairs={{0,16},{4,20},{8,24},{12,28},{16,0},{20,4},{24,8},{28,12},{1,17},{... | collective-permute-start | bytes 442376 | tf_op jit(solution)/shard_map/ppermute | solution.py:37
  32.2 17.9 %collective-permute-start.10 = (bf16[2,4,208,256]{3,2,1,0:T(8,128)(2,1)}, bf16[2,4,208,256]{3,2,1,0:T(8,128)(2,1)}, u32[]{:S(2)}, u32[]{:S(2)}) collective-permute-start(bf16[2,4,208,256]{3,2,1,0:T(8,128)(2,1)} %pad_maximum_fusion), channel_id=1, source_target_pairs={{0,2},{2,0},{1,3},{3,1},{4,6},{6,4},{5,7},{7,5},{8,10},{10,8},{9,1... | collective-permute-start | bytes 2555912 | tf_op jit(solution)/shard_map/ppermute | solution.py:37
  34.8 7.3 %copy-start.27 = (s32[2,4,208,2]{3,2,1,0:T(8,128)}, s32[2,4,208,2]{3,2,1,0:T(8,128)S(1)}, u32[]{:S(2)}) copy-start(s32[2,4,208,2]{3,2,1,0:T(8,128)S(1)} %pad.43.clone) | copy-start | bytes 39940
  37.4 6.6 %copy-start.37 = (bf16[1,2,1,1,1,144,256]{6,5,2,1,0,4,3:T(8,128)(2,1)}, bf16[1,2,1,1,1,144,256]{6,5,2,1,0,4,3:T(8,128)(2,1)S(1)}, u32[]{:S(2)}) copy-start(bf16[1,2,1,1,1,144,256]{6,5,2,1,0,4,3:T(8,128)(2,1)S(1)} %collective-permute-done.3) | copy-start | bytes 442372
  38.1 9.6 %collective-permute-start.4 = (bf16[2,2,1,1,1,144,256]{6,5,2,1,0,4,3:T(8,128)(2,1)}, bf16[2,2,1,1,1,144,256]{6,5,2,1,0,4,3:T(8,128)(2,1)S(1)}, u32[]{:S(2)}, u32[]{:S(2)}) collective-permute-start(bf16[2,2,1,1,1,144,256]{6,5,2,1,0,4,3:T(8,128)(2,1)} %maximum_select_fusion.16), channel_id=1, source_target_pairs={{0,4},{4,0},{8,12},{12,8},{16,20},{20,16},{24,28},{28,24},{1,5},{5... | collective-permute-start | bytes 884744 | tf_op jit(solution)/shard_map/ppermute | solution.py:37
  48.6 19.2 %collective-permute-start.5 = (bf16[2,2,2,1,1,144,256]{6,5,2,1,0,4,3:T(8,128)(2,1)}, bf16[2,2,2,1,1,144,256]{6,5,2,1,0,4,3:T(8,128)(2,1)}, u32[]{:S(2)}, u32[]{:S(2)}) collective-permute-start(bf16[2,2,2,1,1,144,256]{6,5,2,1,0,4,3:T(8,128)(2,1)} %maximum_select_fusion.15), channel_id=1, source_target_pairs={{0,1},{1,0},{2,3},{3,2},{4,5},{5,4},{6,7},{7,6},{8,9},{9,8},{10,11... | collective-permute-start | bytes 1769480 | tf_op jit(solution)/shard_map/ppermute | solution.py:37
  59.9 50.5 %all-to-all-start.1 = ((bf16[16,136,512]{2,1,0:T(8,128)(2,1)}), bf16[16,136,512]{2,1,0:T(8,128)(2,1)S(1)}, u32[]{:S(2)}, u32[]{:S(2)}) async-start(bf16[16,136,512]{2,1,0:T(8,128)(2,1)} %bitcast.253), calls=%async_computation.1 | async-start | bytes 4456448 | tf_op jit(solution)/shard_map/all_to_all | solution.py:702
  67.9 3.3 copy-start.42
  67.9 3.3 copy-start.43
  67.9 3.3 copy-start.44
  69.4 5.2 %collective-permute-start.6 = (bf16[2,2,2,2,1,144,256]{6,5,2,1,0,4,3:T(8,128)(2,1)S(1)}, bf16[2,2,2,2,1,144,256]{6,5,2,1,0,4,3:T(8,128)(2,1)S(1)}, u32[]{:S(2)}, u32[]{:S(2)}) collective-permute-start(bf16[2,2,2,2,1,144,256]{6,5,2,1,0,4,3:T(8,128)(2,1)S(1)} %maximum_select_fusion.11), channel_id=1, source_target_pairs={{0,2},{2,0},{1,3},{3,1},{4,6},{6,4},{5,7},{7,5},{8,10},{10,8},{9,1... | collective-permute-start | bytes 3538952 | tf_op jit(solution)/shard_map/ppermute | solution.py:37
  70.7 2.3 collective-permute-start.1
  71.3 1.7 collective-permute-start.7
  88.5 13.1 %copy-start.10 = (bf16[64,8,2,256]{3,1,2,0:T(8,128)(2,1)}, bf16[64,8,2,256]{3,1,2,0:T(8,128)(2,1)S(1)}, u32[]{:S(2)}) copy-start(bf16[64,8,2,256]{3,1,2,0:T(8,128)(2,1)S(1)} %copy.167) | copy-start | bytes 1572868
  99.2 2.4 collective-permute-start.8
  110.4 100.2 %all-to-all-start = ((bf16[16,136,512]{2,1,0:T(8,128)(2,1)}), bf16[16,136,512]{2,1,0:T(8,128)(2,1)}, u32[]{:S(2)}, u32[]{:S(2)}) async-start(bf16[16,136,512]{2,1,0:T(8,128)(2,1)} %bitcast.252), calls=%async_computation | async-start | bytes 4456448 | tf_op jit(solution)/shard_map/all_to_all | solution.py:702
  121.0 5.2 %copy-start.36 = (bf16[4,1024,256]{2,1,0:T(8,128)(2,1)S(1)}, bf16[4,1024,256]{2,1,0:T(8,128)(2,1)}, u32[]{:S(2)}) copy-start(bf16[4,1024,256]{2,1,0:T(8,128)(2,1)} %param.30) | copy-start | bytes 6291460
  124.2 47.0 %collective-permute-start.13 = (bf16[2,256,1024]{2,1,0:T(8,128)(2,1)}, bf16[2,256,1024]{2,1,0:T(8,128)(2,1)}, u32[]{:S(2)}, u32[]{:S(2)}) collective-permute-start(bf16[2,256,1024]{2,1,0:T(8,128)(2,1)} %get-tuple-element.115), channel_id=1, source_target_pairs={{0,1},{1,0},{2,3},{3,2},{4,5},{5,4},{6,7},{7,6},{8,9},{9,8},{10,11... | collective-permute-start | bytes 3145736 | tf_op jit(solution)/shard_map/ppermute | solution.py:37
  127.6 63.8 %collective-permute-start.11 = (bf16[2,1024,256]{2,1,0:T(8,128)(2,1)}, bf16[2,1024,256]{2,1,0:T(8,128)(2,1)}, u32[]{:S(2)}, u32[]{:S(2)}) collective-permute-start(bf16[2,1024,256]{2,1,0:T(8,128)(2,1)} %get-tuple-element.119), channel_id=1, source_target_pairs={{0,1},{1,0},{2,3},{3,2},{4,5},{5,4},{6,7},{7,6},{8,9},{9,8},{10,11... | collective-permute-start | bytes 3145736 | tf_op jit(solution)/shard_map/ppermute | solution.py:37
  173.7 17.7 %copy-start.34 = (bf16[2,1,1024,256]{3,2,1,0:T(8,128)(2,1)S(1)}, bf16[2,1,1024,256]{3,2,1,0:T(8,128)(2,1)}, u32[]{:S(2)}) copy-start(bf16[2,1,1024,256]{3,2,1,0:T(8,128)(2,1)} %get-tuple-element.118) | copy-start | bytes 3145732
  175.2 19.7 %collective-permute-start.14 = (bf16[2,256,1024]{2,1,0:T(8,128)(2,1)}, bf16[2,256,1024]{2,1,0:T(8,128)(2,1)}, u32[]{:S(2)}, u32[]{:S(2)}) collective-permute-start(bf16[2,256,1024]{2,1,0:T(8,128)(2,1)} %get-tuple-element.113), channel_id=1, source_target_pairs={{0,2},{2,0},{1,3},{3,1},{4,6},{6,4},{5,7},{7,5},{8,10},{10,8},{9,1... | collective-permute-start | bytes 3145736 | tf_op jit(solution)/shard_map/ppermute | solution.py:37
  194.9 4.0 collective-permute-start.12
  194.9 4.0 copy-start.30
  234.1 51.1 %all-to-all-start.3 = ((bf16[16,136,512]{2,1,0:T(8,128)(2,1)}), bf16[16,136,512]{2,1,0:T(8,128)(2,1)}, u32[]{:S(2)}, u32[]{:S(2)}) async-start(bf16[16,136,512]{2,1,0:T(8,128)(2,1)} %bitcast.259), calls=%async_computation.3 | async-start | bytes 4456448 | tf_op jit(solution)/shard_map/all_to_all | solution.py:702
  285.2 137.6 %all-to-all-start.2 = ((bf16[16,136,512]{2,1,0:T(8,128)(2,1)}), bf16[16,136,512]{2,1,0:T(8,128)(2,1)}, u32[]{:S(2)}, u32[]{:S(2)}) async-start(bf16[16,136,512]{2,1,0:T(8,128)(2,1)} %bitcast.251), calls=%async_computation.2 | async-start | bytes 4456448 | tf_op jit(solution)/shard_map/all_to_all | solution.py:702
  306.8 11.2 %collective-permute-start.33 = (bf16[2,1024,256]{2,1,0:T(8,128)(2,1)}, bf16[2,1024,256]{2,1,0:T(8,128)(2,1)}, u32[]{:S(2)}, u32[]{:S(2)}) collective-permute-start(bf16[2,1024,256]{2,1,0:T(8,128)(2,1)} %get-tuple-element.107), channel_id=1, source_target_pairs={{0,2},{2,0},{1,3},{3,1},{4,6},{6,4},{5,7},{7,5},{8,10},{10,8},{9,1... | collective-permute-start | bytes 3145736 | tf_op jit(solution)/shard_map/ppermute | solution.py:37
  318.0 13.5 %collective-permute-start.31 = (bf16[2,256,1024]{2,1,0:T(8,128)(2,1)}, bf16[2,256,1024]{2,1,0:T(8,128)(2,1)}, u32[]{:S(2)}, u32[]{:S(2)}) collective-permute-start(bf16[2,256,1024]{2,1,0:T(8,128)(2,1)} %get-tuple-element.111), channel_id=1, source_target_pairs={{0,2},{2,0},{1,3},{3,1},{4,6},{6,4},{5,7},{7,5},{8,10},{10,8},{9,1... | collective-permute-start | bytes 3145736 | tf_op jit(solution)/shard_map/ppermute | solution.py:37
  321.5 36.9 %collective-permute-start.34 = (bf16[2,1024,256]{2,1,0:T(8,128)(2,1)}, bf16[2,1024,256]{2,1,0:T(8,128)(2,1)}, u32[]{:S(2)}, u32[]{:S(2)}) collective-permute-start(bf16[2,1024,256]{2,1,0:T(8,128)(2,1)} %get-tuple-element.105), channel_id=1, source_target_pairs={{0,1},{1,0},{2,3},{3,2},{4,5},{5,4},{6,7},{7,6},{8,9},{9,8},{10,11... | collective-permute-start | bytes 3145736 | tf_op jit(solution)/shard_map/ppermute | solution.py:37
  329.9 37.3 %collective-permute-start.18 = (bf16[832,512]{1,0:T(8,128)(2,1)}, bf16[832,512]{1,0:T(8,128)(2,1)}, u32[]{:S(2)}, u32[]{:S(2)}) collective-permute-start(bf16[832,512]{1,0:T(8,128)(2,1)} %shard_map.272), channel_id=1, source_target_pairs={{0,2},{2,0},{1,3},{3,1},{4,6},{6,4},{5,7},{7,5},{8,10},{10,8},{9,1... | collective-permute-start | bytes 2555912 | tf_op jit(solution)/shard_map/ppermute | solution.py:37
  334.1 24.2 %copy-start.33 = (bf16[2,1,1024,256]{3,2,1,0:T(8,128)(2,1)S(1)}, bf16[2,1,1024,256]{3,2,1,0:T(8,128)(2,1)}, u32[]{:S(2)}) copy-start(bf16[2,1,1024,256]{3,2,1,0:T(8,128)(2,1)} %get-tuple-element.104) | copy-start | bytes 3145732
  335.6 84.0 %collective-permute-start.32 = (bf16[2,256,1024]{2,1,0:T(8,128)(2,1)}, bf16[2,256,1024]{2,1,0:T(8,128)(2,1)}, u32[]{:S(2)}, u32[]{:S(2)}) collective-permute-start(bf16[2,256,1024]{2,1,0:T(8,128)(2,1)} %get-tuple-element.109), channel_id=1, source_target_pairs={{0,1},{1,0},{2,3},{3,2},{4,5},{5,4},{6,7},{7,6},{8,9},{9,8},{10,11... | collective-permute-start | bytes 3145736 | tf_op jit(solution)/shard_map/ppermute | solution.py:37
  361.7 5.5 %copy-start.11 = (bf16[64,8,2,256]{3,1,2,0:T(8,128)(2,1)S(1)}, bf16[64,8,2,256]{3,1,2,0:T(8,128)(2,1)}, u32[]{:S(2)}) copy-start(bf16[64,8,2,256]{3,1,2,0:T(8,128)(2,1)} %copy-done.10) | copy-start | bytes 1572868
  361.7 5.5 %copy-start.12 = (bf16[4,208,512]{2,1,0:T(8,128)(2,1)S(1)}, bf16[4,208,512]{2,1,0:T(8,128)(2,1)}, u32[]{:S(2)}) copy-start(bf16[4,208,512]{2,1,0:T(8,128)(2,1)} %get-tuple-element.120.cot_ref) | copy-start | bytes 2555908
  361.7 5.5 %copy-start.15 = (bf16[4,208,512]{2,1,0:T(8,128)(2,1)S(1)}, bf16[4,208,512]{2,1,0:T(8,128)(2,1)}, u32[]{:S(2)}) copy-start(bf16[4,208,512]{2,1,0:T(8,128)(2,1)} %copy-done.14) | copy-start | bytes 2555908
  361.7 5.5 %copy-start.19 = (f32[4,208,128]{2,1,0:T(8,128)S(1)}, f32[4,208,128]{2,1,0:T(8,128)}, u32[]{:S(2)}) copy-start(f32[4,208,128]{2,1,0:T(8,128)} %copy-done.18) | copy-start | bytes 1277956
  414.1 5.4 %copy-start.21 = (bf16[8,2,2,144,256]{4,3,2,1,0:T(8,128)(2,1)}, bf16[8,2,2,144,256]{4,3,2,1,0:T(8,128)(2,1)S(1)}, u32[]{:S(2)}) copy-start(bf16[8,2,2,144,256]{4,3,2,1,0:T(8,128)(2,1)S(1)} %pad.48) | copy-start | bytes 7077892
  415.3 4.4 copy-start.31
  415.3 33.1 %collective-permute-start.26 = (bf16[2,2,2,2,1,144,256]{6,5,4,3,2,1,0:T(8,128)(2,1)}, bf16[2,2,2,2,1,144,256]{6,5,4,3,2,1,0:T(8,128)(2,1)}, u32[]{:S(2)}, u32[]{:S(2)}) collective-permute-start(bf16[2,2,2,2,1,144,256]{6,5,4,3,2,1,0:T(8,128)(2,1)} %constant_dynamic-slice_fusion.9), channel_id=1, source_target_pairs={{0,2},{2,0},{1,3},{3,1},{4,6},{6,4},{5,7},{7,5},{8,10},{10,8},{9,1... | collective-permute-start | bytes 3538952 | tf_op jit(solution)/shard_map/ppermute | solution.py:37
  419.5 9.0 %collective-permute-start.21 = (f32[4,512]{1,0:T(4,128)S(1)}, f32[4,512]{1,0:T(4,128)S(1)}, u32[]{:S(2)}, u32[]{:S(2)}) collective-permute-start(f32[4,512]{1,0:T(4,128)S(1)} %slice.146), channel_id=1, source_target_pairs={{0,2},{2,0},{1,3},{3,1},{4,6},{6,4},{5,7},{7,5},{8,10},{10,8},{9,1... | collective-permute-start | bytes 24584 | tf_op jit(solution)/shard_map/ppermute | solution.py:37
  422.8 6.3 %copy-start.24 = (bf16[2,2,256,1024]{3,2,1,0:T(8,128)(2,1)S(1)}, bf16[2,2,256,1024]{3,2,1,0:T(8,128)(2,1)}, u32[]{:S(2)}) copy-start(bf16[2,2,256,1024]{3,2,1,0:T(8,128)(2,1)} %maximum_select_fusion.6) | copy-start | bytes 6291460
  428.1 23.6 %collective-permute-start.15 = (bf16[832,512]{1,0:T(8,128)(2,1)}, bf16[832,512]{1,0:T(8,128)(2,1)}, u32[]{:S(2)}, u32[]{:S(2)}) collective-permute-start(bf16[832,512]{1,0:T(8,128)(2,1)} %shard_map.270), channel_id=1, source_target_pairs={{0,2},{2,0},{1,3},{3,1},{4,6},{6,4},{5,7},{7,5},{8,10},{10,8},{9,1... | collective-permute-start | bytes 2555912 | tf_op jit(solution)/shard_map/ppermute | solution.py:37
  428.5 8.8 %collective-permute-start.22 = (f32[4,512]{1,0:T(4,128)S(1)}, f32[4,512]{1,0:T(4,128)S(1)}, u32[]{:S(2)}, u32[]{:S(2)}) collective-permute-start(f32[4,512]{1,0:T(4,128)S(1)} %slice_add_fusion), channel_id=1, source_target_pairs={{0,1},{1,0},{2,3},{3,2},{4,5},{5,4},{6,7},{7,6},{8,9},{9,8},{10,11... | collective-permute-start | bytes 24584 | tf_op jit(solution)/shard_map/ppermute | solution.py:37
  431.8 4.4 copy-start.17
  437.3 4.5 collective-permute-start.23
  438.4 9.9 %copy-start.22 = (bf16[8,2,2,144,256]{4,3,2,1,0:T(8,128)(2,1)S(1)}, bf16[8,2,2,144,256]{4,3,2,1,0:T(8,128)(2,1)}, u32[]{:S(2)}) copy-start(bf16[8,2,2,144,256]{4,3,2,1,0:T(8,128)(2,1)} %copy-done.21) | copy-start | bytes 7077892
  441.8 26.1 %collective-permute-start.19 = (bf16[788,256]{1,0:T(8,128)(2,1)}, bf16[788,256]{1,0:T(8,128)(2,1)}, u32[]{:S(2)}, u32[]{:S(2)}) collective-permute-start(bf16[788,256]{1,0:T(8,128)(2,1)} %bitcast.246), channel_id=1, source_target_pairs={{0,2},{2,0},{1,3},{3,1},{4,6},{6,4},{5,7},{7,5},{8,10},{10,8},{9,1... | collective-permute-start | bytes 1210376 | tf_op jit(solution)/shard_map/ppermute | solution.py:37
  441.9 9.8 %copy-start.29 = (f32[4,208,512]{2,1,0:T(8,128)S(1)}, f32[4,208,512]{2,1,0:T(8,128)}, u32[]{:S(2)}) copy-start(f32[4,208,512]{2,1,0:T(8,128)} %get-tuple-element.29.mid_ref) | copy-start | bytes 5111812
  441.9 15.5 %collective-permute-start.24 = (f32[4,512]{1,0:T(4,128)S(1)}, f32[4,512]{1,0:T(4,128)S(1)}, u32[]{:S(2)}, u32[]{:S(2)}) collective-permute-start(f32[4,512]{1,0:T(4,128)S(1)} %add.235), channel_id=1, source_target_pairs={{0,16},{4,20},{8,24},{12,28},{16,0},{20,4},{24,8},{28,12},{1,17},{... | collective-permute-start | bytes 24584 | tf_op jit(solution)/shard_map/ppermute | solution.py:37
  450.0 15.7 %collective-permute-start.27 = (bf16[2,2,2,1,1,144,256]{6,5,4,3,2,1,0:T(8,128)(2,1)S(1)}, bf16[2,2,2,1,1,144,256]{6,5,4,3,2,1,0:T(8,128)(2,1)}, u32[]{:S(2)}, u32[]{:S(2)}) collective-permute-start(bf16[2,2,2,1,1,144,256]{6,5,4,3,2,1,0:T(8,128)(2,1)S(1)} %constant_dynamic-slice_fusion.8), channel_id=1, source_target_pairs={{0,1},{1,0},{2,3},{3,2},{4,5},{5,4},{6,7},{7,6},{8,9},{9,8},{10,11... | collective-permute-start | bytes 1769480 | tf_op jit(solution)/shard_map/ppermute | solution.py:37
  457.3 3.7 collective-permute-start.25
  459.1 8.9 %copy-start.35 = (bf16[788,1,256]{2,1,0:T(2,128)(2,1)S(1)}, bf16[788,1,256]{2,1,0:T(2,128)(2,1)}, u32[]{:S(2)}) copy-start(bf16[788,1,256]{2,1,0:T(2,128)(2,1)} %get-tuple-element.135) | copy-start | bytes 1210372
  459.2 11.5 %collective-permute-start.16 = (bf16[788,256]{1,0:T(8,128)(2,1)S(1)}, bf16[788,256]{1,0:T(8,128)(2,1)S(1)}, u32[]{:S(2)}, u32[]{:S(2)}) collective-permute-start(bf16[788,256]{1,0:T(8,128)(2,1)S(1)} %bitcast.287), channel_id=1, source_target_pairs={{0,2},{2,0},{1,3},{3,1},{4,6},{6,4},{5,7},{7,5},{8,10},{10,8},{9,1... | collective-permute-start | bytes 1210376 | tf_op jit(solution)/shard_map/ppermute | solution.py:37
  466.9 8.4 %collective-permute-start.28 = (bf16[2,2,1,1,1,144,256]{6,5,4,3,2,1,0:T(8,128)(2,1)S(1)}, bf16[2,2,1,1,1,144,256]{6,5,4,3,2,1,0:T(8,128)(2,1)S(1)}, u32[]{:S(2)}, u32[]{:S(2)}) collective-permute-start(bf16[2,2,1,1,1,144,256]{6,5,4,3,2,1,0:T(8,128)(2,1)S(1)} %constant_dynamic-slice_fusion.7), channel_id=1, source_target_pairs={{0,4},{4,0},{8,12},{12,8},{16,20},{20,16},{24,28},{28,24},{1,5},{5... | collective-permute-start | bytes 884744 | tf_op jit(solution)/shard_map/ppermute | solution.py:37
  469.1 12.4 %collective-permute-start.20 = (bf16[788,256]{1,0:T(8,128)(2,1)S(1)}, bf16[788,256]{1,0:T(8,128)(2,1)S(1)}, u32[]{:S(2)}, u32[]{:S(2)}) collective-permute-start(bf16[788,256]{1,0:T(8,128)(2,1)S(1)} %get-tuple-element.128), channel_id=1, source_target_pairs={{0,1},{1,0},{2,3},{3,2},{4,5},{5,4},{6,7},{7,6},{8,9},{9,8},{10,11... | collective-permute-start | bytes 1210376 | tf_op jit(solution)/shard_map/ppermute | solution.py:37
  470.8 17.5 %collective-permute-start.17 = (bf16[788,256]{1,0:T(8,128)(2,1)S(1)}, bf16[788,256]{1,0:T(8,128)(2,1)S(1)}, u32[]{:S(2)}, u32[]{:S(2)}) collective-permute-start(bf16[788,256]{1,0:T(8,128)(2,1)S(1)} %get-tuple-element.130), channel_id=1, source_target_pairs={{0,1},{1,0},{2,3},{3,2},{4,5},{5,4},{6,7},{7,6},{8,9},{9,8},{10,11... | collective-permute-start | bytes 1210376 | tf_op jit(solution)/shard_map/ppermute | solution.py:37
  475.5 8.1 %collective-permute-start.29 = (bf16[1,2,1,1,1,144,256]{6,5,4,3,2,1,0:T(8,128)(2,1)S(1)}, bf16[1,2,1,1,1,144,256]{6,5,4,3,2,1,0:T(8,128)(2,1)S(1)}, u32[]{:S(2)}, u32[]{:S(2)}) collective-permute-start(bf16[1,2,1,1,1,144,256]{6,5,4,3,2,1,0:T(8,128)(2,1)S(1)} %constant_dynamic-slice_fusion.6), channel_id=1, source_target_pairs={{0,16},{4,20},{8,24},{12,28},{16,0},{20,4},{24,8},{28,12},{1,17},{... | collective-permute-start | bytes 442376 | tf_op jit(solution)/shard_map/ppermute | solution.py:37
  483.6 10.1 %copy-start.1 = (s32[2,1576,2]{1,2,0:T(2,128)S(1)}, s32[2,1576,2]{1,2,0:T(2,128)}, u32[]{:S(2)}) copy-start(s32[2,1576,2]{1,2,0:T(2,128)} %param.18) | copy-start | bytes 75652
  483.7 6.2 %collective-permute-start.30 = (bf16[1,1,1,1,1,144,256]{6,5,4,3,2,1,0:T(8,128)(2,1)S(1)}, bf16[1,1,1,1,1,144,256]{6,5,4,3,2,1,0:T(8,128)(2,1)S(1)}, u32[]{:S(2)}, u32[]{:S(2)}) collective-permute-start(bf16[1,1,1,1,1,144,256]{6,5,4,3,2,1,0:T(8,128)(2,1)S(1)} %constant_dynamic-slice_fusion.5), channel_id=1, source_target_pairs={{0,8},{4,12},{8,0},{12,4},{16,24},{20,28},{24,16},{28,20},{1,9},{5... | collective-permute-start | bytes 221192 | tf_op jit(solution)/shard_map/ppermute | solution.py:37
  (23 other events, 39.7 us)
